TPU v7x, 32 devices: a whole 2x2x4 slice. The times are simulated.
32 devices in a mesh: dp: 8 (over y, x, core), tensor: 4 (over z).
Axes of the slice: x: 2, y: 2, z: 4, core: 2. Of those that a mesh axis runs over, the one named last changes fastest.
Arguments:
- hidden: bfloat16 [4096, 2048], P(('dp', 'tensor')), may hold values from -6 to 6
- cotangent: bfloat16 [4096, 2048], P(('dp', 'tensor')), may hold values from -6 to 6
- routes: int32 [4096, 6], P('dp'), may hold values from 0 to 15, all different within a row; in each aligned block of 512 rows (0 to 511, 512 to 1023, ...) at most 256 rows name the same one
- route_gates: float32 [4096, 6], P('dp'), may hold values from 0.08 to 0.32
- doc_lengths: int32 [8, 3], P('dp'), may hold values from 1 to 448, 512 in all within a row
- attn_gain: float32 [2048], replicated, may hold values from 0.25 to 1.75
- query_weight: bfloat16 [2048, 3072], P('dp', 'tensor'), may hold values from -0.125 to 0.125
- latent_weight: bfloat16 [2048, 576], replicated, may hold values from -0.125 to 0.125
- latent_gain: float32 [512], replicated, may hold values from 0.25 to 1.75
- expand_weight: bfloat16 [512, 4096], P('dp', 'tensor'), may hold values from -0.25 to 0.25
- output_weight: bfloat16 [2048, 2048], P('tensor', 'dp'), may hold values from -2 to 2
- mlp_gain: float32 [2048], replicated, may hold values from 0.25 to 1.75
- shared_gate: bfloat16 [2048, 2816], P('dp', 'tensor'), may hold values from -0.125 to 0.125
- shared_up: bfloat16 [2048, 2816], P('dp', 'tensor'), may hold values from -0.125 to 0.125
- shared_down: bfloat16 [2816, 2048], P('tensor', 'dp'), may hold values from -0.109375 to 0.109375
- expert_gate: bfloat16 [16, 2048, 1408], P('dp', None, 'tensor'), may hold values from -0.125 to 0.125
- expert_up: bfloat16 [16, 2048, 1408], P('dp', None, 'tensor'), may hold values from -0.125 to 0.125
- expert_down: bfloat16 [16, 1408, 2048], P('dp', 'tensor'), may hold values from -0.15625 to 0.15625
Outputs:
- layer_out: bfloat16 [4096, 2048], P(('dp', 'tensor'))
- hidden_grad: float32 [4096, 2048], P(('dp', 'tensor'))
- attngain_grad: float32 [2048], replicated
- query_grad: float32 [2048, 3072], P('dp', 'tensor')
- latent_grad: float32 [2048, 576], replicated
- latgain_grad: float32 [512], replicated
- expand_grad: float32 [512, 4096], P('dp', 'tensor')
- output_grad: float32 [2048, 2048], P('tensor', 'dp')
- mlpgain_grad: float32 [2048], replicated
- sgate_grad: float32 [2048, 2816], P('dp', 'tensor')
- sup_grad: float32 [2048, 2816], P('dp', 'tensor')
- sdown_grad: float32 [2816, 2048], P('tensor', 'dp')
- egate_grad: float32 [16, 2048, 1408], P('dp', None, 'tensor')
- eup_grad: float32 [16, 2048, 1408], P('dp', None, 'tensor')
- edown_grad: float32 [16, 1408, 2048], P('dp', 'tensor')
Inputs may be any that keep to these rules, and one draw needn't show every extreme that they name: `routes`: the 6 experts of a token differ. Within each group of 512 rows no expert is named by more than 256 rows, a bound that some block reaches. `doc_lengths`: each row sums to 512; its longest document has exactly 448 tokens.
All inputs are finite; a program needn't handle non-finite values.
Results may differ from a plain program's by a relative error of at most 0.018.
Values may be sent and summed in bfloat16 or wider, within the bound.
A program may use at most 448 MiB of HBM per device.

v0:
```python
import functools
from types import SimpleNamespace

import jax
import jax.numpy as jnp
from jax import lax
from jax.experimental import pallas as pl
from jax.experimental.pallas import tpu as pltpu
from jax.sharding import PartitionSpec as P

DP = "dp"
TENSOR = "tensor"
NOPE = 128
ROPE = 64
VDIM = 128
LATENT = 512
TOPK = 6

(
    K_RING,
    K_X,
    K_Y,
    K_CORE,
    K_FAR_Y,
    K_FAR_X,
    K_CORE_X,
    K_CORE_Y,
    K_CORE_FAR,
    K_CORE_OWN,
    K_X_FIRST,
    K_X_LAST,
    K_Y_FIRST,
    K_Y_LAST,
    K_FAR_RING,
) = range(15)


epsilon = 1e-06
rope_base = 10000.0


def bfloat(values):
    return values.astype(jnp.bfloat16)


def plain_dot(left_op, right_op):
    return jnp.dot(left_op, right_op, preferred_element_type=jnp.float32)


def first_dot(left_op, right_op):
    return lax.dot_general(
        left_op, right_op, (((0,), (0,)), ((), ())), preferred_element_type=jnp.float32
    )


def last_dot(left_op, right_op):
    return lax.dot_general(
        left_op, right_op, (((1,), (1,)), ((), ())), preferred_element_type=jnp.float32
    )


def rms_scale(values):
    return lax.rsqrt(jnp.mean(values * values, axis=-1, keepdims=True) + epsilon)


def rms_back(grad_out, values, scaling, gain_vec):
    scaled_grad = grad_out * gain_vec
    inner_sum = jnp.mean(scaled_grad * values, axis=-1, keepdims=True)
    grad_in = scaling * scaled_grad - values * (scaling * scaling * scaling) * inner_sum
    return (grad_in, jnp.sum(grad_out * values * scaling, axis=0))


def silu_parts(values):
    sigmoid = jax.nn.sigmoid(values)
    return (values * sigmoid, sigmoid * (1.0 + values * (1.0 - sigmoid)))


def rope_tables(positions, rot_width):
    middle = rot_width // 2
    frequency = rope_base ** (-jnp.arange(middle, dtype=jnp.float32) * 2.0 / rot_width)
    angles = positions.astype(jnp.float32)[:, None] * frequency[None, :]
    return (jnp.cos(angles), jnp.sin(angles))


def rotate(values, cos_table, sin_table):
    middle = values.shape[-1] // 2
    first_half = values[..., :middle]
    second_half = values[..., middle:]
    return jnp.concatenate(
        [
            first_half * cos_table - second_half * sin_table,
            second_half * cos_table + first_half * sin_table,
        ],
        axis=-1,
    )


def doc_layout(lengths, row_count):
    doc_ends = jnp.cumsum(lengths)
    tok_index = jnp.arange(row_count, dtype=jnp.int32)
    before = (doc_ends[None, :] <= tok_index[:, None]).astype(jnp.int32)
    doc_ids = jnp.sum(before, axis=1)
    starts = jnp.sum(before * lengths[None, :], axis=1)
    return (doc_ids, tok_index - starts)


def slot_tables(routes, experts, capacity):
    row_count = routes.shape[0] * routes.shape[1]
    flat_routes = routes.reshape(row_count)
    onehot = (flat_routes[:, None] == jnp.arange(experts, dtype=jnp.int32)[None, :]).astype(
        jnp.int32
    )
    earlier = jnp.cumsum(onehot, axis=0) - onehot
    position = jnp.sum(earlier * onehot, axis=1)
    slot_ids = flat_routes * capacity + position
    tok_rows = jnp.arange(row_count, dtype=jnp.int32) // routes.shape[1]
    owner_tok = jnp.zeros((experts * capacity,), jnp.int32).at[slot_ids].set(tok_rows)
    return (slot_ids.reshape(routes.shape), owner_tok)


def slot_share(capacity):
    return (0, capacity)


def route_rows(outgoing, apply_fn):
    arrived = lax.all_to_all(outgoing, DP, split_axis=1, concat_axis=1, tiled=True)
    result, extra = apply_fn(arrived)
    back = lax.all_to_all(
        result.astype(jnp.bfloat16), DP, split_axis=1, concat_axis=1, tiled=True
    ).astype(result.dtype)
    return (back, extra)


def block_mask(doc_ids, row_start, block_rows):
    group_rows = doc_ids.shape[0]
    key_index = jnp.arange(group_rows, dtype=jnp.int32)
    query_index = row_start + jnp.arange(block_rows, dtype=jnp.int32)
    return (key_index[None, :] <= query_index[:, None]) & (doc_ids[None, :] == doc_ids[:, None])


def attend(query_all, key_all, value_all, doc_ids, scaling):
    group_rows = query_all.shape[0]
    block_rows = min(512, group_rows)
    block_count = group_rows // block_rows

    def one_block(block_id):
        row_start = block_id * block_rows
        allowed = block_mask(doc_ids, row_start, block_rows)
        scores = (
            jnp.einsum("qhd,khd->hqk", query_all, key_all, preferred_element_type=jnp.float32)
            * scaling
        )
        scores = jnp.where(allowed[None], scores, -jnp.inf)
        row_max = jnp.max(scores, axis=-1, keepdims=True)
        exp_scores = jnp.exp(scores - row_max)
        row_total = jnp.sum(exp_scores, axis=-1, keepdims=True)
        probability = bfloat(exp_scores / row_total)
        output = jnp.einsum(
            "hqk,khd->qhd", probability, value_all, preferred_element_type=jnp.float32
        )
        return (output, (row_max + jnp.log(row_total))[..., 0])

    outputs, log_total = lax.map(one_block, jnp.arange(block_count, dtype=jnp.int32))
    return (outputs.reshape(group_rows, outputs.shape[2], outputs.shape[3]), log_total)


def attend_back(query_all, key_all, value_all, doc_ids, scaling, log_total, grad_out):
    group_rows = query_all.shape[0]
    block_rows = min(512, group_rows)
    block_count = group_rows // block_rows

    def one_block(carried, inputs):
        key_grad, value_grad = carried
        block_id, block_lse = inputs
        row_start = block_id * block_rows
        allowed = block_mask(doc_ids, row_start, block_rows)
        scores = (
            jnp.einsum("qhd,khd->hqk", query_all, key_all, preferred_element_type=jnp.float32)
            * scaling
        )
        scores = jnp.where(allowed[None], scores, -jnp.inf)
        probability = jnp.exp(scores - block_lse[..., None])
        value_grad = value_grad + jnp.einsum(
            "hqk,qhd->khd", bfloat(probability), grad_out, preferred_element_type=jnp.float32
        )
        prob_grad = jnp.einsum(
            "qhd,khd->hqk", grad_out, value_all, preferred_element_type=jnp.float32
        )
        row_dot = jnp.sum(prob_grad * probability, axis=-1, keepdims=True)
        score_grad = bfloat(probability * (prob_grad - row_dot))
        query_grad = (
            jnp.einsum("hqk,khd->qhd", score_grad, key_all, preferred_element_type=jnp.float32)
            * scaling
        )
        key_grad = (
            key_grad
            + jnp.einsum("hqk,qhd->khd", score_grad, query_all, preferred_element_type=jnp.float32)
            * scaling
        )
        return ((key_grad, value_grad), query_grad)

    start_state = (jnp.zeros(key_all.shape, jnp.float32), jnp.zeros(value_all.shape, jnp.float32))
    (key_grad, value_grad), query_blocks = lax.scan(
        one_block, start_state, (jnp.arange(block_count, dtype=jnp.int32), log_total)
    )
    query_grad = query_blocks.reshape(group_rows, query_blocks.shape[2], query_blocks.shape[3])
    return (query_grad, key_grad, value_grad)


def forward_pass(
    hidden,
    cotangent,
    routes,
    route_gates,
    doc_lengths,
    attn_gain,
    query_weight,
    latent_weight,
    latent_gain,
    expand_weight,
    output_weight,
    mlp_gain,
    shared_gate,
    shared_up,
    shared_down,
    expert_gate,
    expert_up,
    expert_down,
):
    tensor_count = lax.axis_size(TENSOR)
    dp_count = lax.axis_size(DP)
    local_rows = hidden.shape[0]
    group_rows = local_rows * tensor_count
    query_full, expand_full, output_full, sgate_full, sup_full, sdown_full = (
        lax.all_gather(query_weight, DP, axis=0, tiled=True),
        lax.all_gather(expand_weight, DP, axis=0, tiled=True),
        lax.all_gather(output_weight, DP, axis=1, tiled=True),
        lax.all_gather(shared_gate, DP, axis=0, tiled=True),
        lax.all_gather(shared_up, DP, axis=0, tiled=True),
        lax.all_gather(shared_down, DP, axis=1, tiled=True),
    )
    hidden_f = hidden.astype(jnp.float32)
    scale_one = rms_scale(hidden_f)
    normed_one = bfloat(hidden_f * scale_one * attn_gain)
    latent_full = plain_dot(normed_one, latent_weight)
    latent_part = latent_full[:, :LATENT]
    scale_latent = rms_scale(latent_part)
    latent_norm = bfloat(latent_part * scale_latent * latent_gain)
    doc_ids, positions = doc_layout(doc_lengths[0], group_rows)
    cos_group, sin_group = rope_tables(positions, ROPE)
    local_start = lax.axis_index(TENSOR) * local_rows
    cos_local = lax.dynamic_slice_in_dim(cos_group, local_start, local_rows, 0)
    sin_local = lax.dynamic_slice_in_dim(sin_group, local_start, local_rows, 0)
    key_rot = bfloat(rotate(latent_full[:, LATENT:], cos_local, sin_local))
    normed_group, latent_group, keyrot_group = (
        lax.all_gather(normed_one, TENSOR, axis=0, tiled=True),
        lax.all_gather(latent_norm, TENSOR, axis=0, tiled=True),
        lax.all_gather(key_rot, TENSOR, axis=0, tiled=True),
    )
    local_heads = query_full.shape[1] // (NOPE + ROPE)
    query_raw = plain_dot(normed_group, query_full).reshape(group_rows, local_heads, NOPE + ROPE)
    query_rot = rotate(query_raw[..., NOPE:], cos_group[:, None, :], sin_group[:, None, :])
    query_all = bfloat(jnp.concatenate([query_raw[..., :NOPE], query_rot], axis=-1))
    expanded = plain_dot(latent_group, expand_full).reshape(group_rows, local_heads, NOPE + VDIM)
    key_shared = jnp.broadcast_to(keyrot_group[:, None, :], (group_rows, local_heads, ROPE))
    key_all = jnp.concatenate([bfloat(expanded[..., :NOPE]), key_shared], axis=-1)
    value_all = bfloat(expanded[..., NOPE:])
    scaling = (NOPE + ROPE) ** (-0.5)
    attended, log_total = attend(query_all, key_all, value_all, doc_ids, scaling)
    attended_low = bfloat(attended).reshape(group_rows, local_heads * VDIM)
    attn_local = lax.psum_scatter(
        plain_dot(attended_low, output_full), TENSOR, scatter_dimension=0, tiled=True
    )
    residual = hidden_f + attn_local
    scale_two = rms_scale(residual)
    normed_two = bfloat(residual * scale_two * mlp_gain)
    mlp_rows, cotan_rows = (
        lax.all_gather(normed_two, TENSOR, axis=0, tiled=True),
        lax.all_gather(cotangent, TENSOR, axis=0, tiled=True),
    )
    shared_gpre = plain_dot(mlp_rows, sgate_full)
    shared_upre = plain_dot(mlp_rows, sup_full)
    shared_silu, shared_dsilu = silu_parts(shared_gpre)
    shared_hidden = bfloat(shared_silu * shared_upre)
    shared_out = plain_dot(shared_hidden, sdown_full)
    local_experts = expert_gate.shape[0]
    experts = local_experts * dp_count
    capacity = group_rows * TOPK * 4 // (3 * experts)
    slot_ids, owner_tok = slot_tables(routes, experts, capacity)
    slot_start, slot_count = slot_share(capacity)
    all_tok = owner_tok.reshape(dp_count, local_experts, capacity).transpose(1, 0, 2)
    send_rows = mlp_rows[all_tok]

    def expert_apply(received):
        gate_pre = jnp.einsum(
            "jscd,jdf->jscf", received, expert_gate, preferred_element_type=jnp.float32
        )
        up_pre = jnp.einsum(
            "jscd,jdf->jscf", received, expert_up, preferred_element_type=jnp.float32
        )
        gate_silu, gate_dsilu = silu_parts(gate_pre)
        activated = bfloat(gate_silu * up_pre)
        result = jnp.einsum(
            "jscf,jfd->jscd", activated, expert_down, preferred_element_type=jnp.float32
        )
        return (result, (received, up_pre, gate_silu, gate_dsilu, activated))

    returned, expert_state = route_rows(send_rows, expert_apply)
    received, up_pre, gate_silu, gate_dsilu, activated = expert_state
    position = slot_ids % capacity - slot_start
    slot_mask = ((position >= 0) & (position < slot_count)).astype(jnp.float32)
    flat_index = (
        routes % local_experts * dp_count + routes // local_experts
    ) * slot_count + jnp.clip(position, 0, slot_count - 1)
    returned_flat = returned.reshape(local_experts * dp_count * slot_count, returned.shape[-1])
    routed = jnp.sum((route_gates * slot_mask)[:, :, None] * returned_flat[flat_index], axis=1)
    moe_local = lax.psum_scatter(
        (shared_out + routed).astype(jnp.bfloat16), TENSOR, scatter_dimension=0, tiled=True
    ).astype(jnp.float32)
    layer_out = bfloat(residual + moe_local)
    return SimpleNamespace(
        layer_out=layer_out,
        hidden_f=hidden_f,
        scale_one=scale_one,
        normed_one=normed_one,
        latent_part=latent_part,
        scale_latent=scale_latent,
        cos_local=cos_local,
        sin_local=sin_local,
        cos_group=cos_group,
        sin_group=sin_group,
        doc_ids=doc_ids,
        normed_group=normed_group,
        latent_group=latent_group,
        query_all=query_all,
        key_all=key_all,
        value_all=value_all,
        log_total=log_total,
        attended_low=attended_low,
        residual=residual,
        scale_two=scale_two,
        mlp_rows=mlp_rows,
        cotan_rows=cotan_rows,
        shared_upre=shared_upre,
        shared_silu=shared_silu,
        shared_dsilu=shared_dsilu,
        shared_hidden=shared_hidden,
        slot_ids=slot_ids,
        send_tok=all_tok,
        flat_index=flat_index,
        slot_mask=slot_mask,
        received=received,
        up_pre=up_pre,
        gate_silu=gate_silu,
        gate_dsilu=gate_dsilu,
        activated=activated,
        query_full=query_full,
        expand_full=expand_full,
        output_full=output_full,
        sgate_full=sgate_full,
        sup_full=sup_full,
        sdown_full=sdown_full,
    )


def general_shards(
    hidden,
    cotangent,
    routes,
    route_gates,
    doc_lengths,
    attn_gain,
    query_weight,
    latent_weight,
    latent_gain,
    expand_weight,
    output_weight,
    mlp_gain,
    shared_gate,
    shared_up,
    shared_down,
    expert_gate,
    expert_up,
    expert_down,
):
    kept_state = forward_pass(
        hidden,
        cotangent,
        routes,
        route_gates,
        doc_lengths,
        attn_gain,
        query_weight,
        latent_weight,
        latent_gain,
        expand_weight,
        output_weight,
        mlp_gain,
        shared_gate,
        shared_up,
        shared_down,
        expert_gate,
        expert_up,
        expert_down,
    )
    dp_count = lax.axis_size(DP)
    local_experts = expert_gate.shape[0]
    experts = local_experts * dp_count
    group_rows = kept_state.mlp_rows.shape[0]
    capacity = group_rows * TOPK * 4 // (3 * experts)
    cotan_rows = kept_state.cotan_rows
    mlp_rows = kept_state.mlp_rows
    sdown_wgrad = first_dot(kept_state.shared_hidden, cotan_rows)
    shared_hgrad = last_dot(cotan_rows, kept_state.sdown_full)
    sgate_pgrad = bfloat(shared_hgrad * kept_state.shared_upre * kept_state.shared_dsilu)
    sup_pgrad = bfloat(shared_hgrad * kept_state.shared_silu)
    sgate_wgrad = first_dot(mlp_rows, sgate_pgrad)
    sup_wgrad = first_dot(mlp_rows, sup_pgrad)
    mlp_partial = last_dot(sgate_pgrad, kept_state.sgate_full) + last_dot(
        sup_pgrad, kept_state.sup_full
    )
    slot_start, slot_count = slot_share(capacity)
    slot_gate = (
        jnp.zeros((experts * capacity,), jnp.float32)
        .at[kept_state.slot_ids.reshape(-1)]
        .set(route_gates.reshape(-1))
    )
    all_gate = slot_gate.reshape(dp_count, local_experts, capacity).transpose(1, 0, 2)
    grad_send = bfloat(all_gate[..., None] * cotan_rows[kept_state.send_tok].astype(jnp.float32))
    received = kept_state.received

    def expert_back(grad_recv):
        expert_down_partial = jnp.einsum(
            "jscf,jscd->jfd", kept_state.activated, grad_recv, preferred_element_type=jnp.float32
        )
        act_grad = jnp.einsum(
            "jscd,jfd->jscf", grad_recv, expert_down, preferred_element_type=jnp.float32
        )
        gate_pgrad = bfloat(act_grad * kept_state.up_pre * kept_state.gate_dsilu)
        up_pgrad = bfloat(act_grad * kept_state.gate_silu)
        row_gradient = jnp.einsum(
            "jscf,jdf->jscd", gate_pgrad, expert_gate, preferred_element_type=jnp.float32
        )
        row_gradient = row_gradient + jnp.einsum(
            "jscf,jdf->jscd", up_pgrad, expert_up, preferred_element_type=jnp.float32
        )
        expert_gate_partial = jnp.einsum(
            "jscd,jscf->jdf", received, gate_pgrad, preferred_element_type=jnp.float32
        )
        expert_up_partial = jnp.einsum(
            "jscd,jscf->jdf", received, up_pgrad, preferred_element_type=jnp.float32
        )
        return (row_gradient, (expert_gate_partial, expert_up_partial, expert_down_partial))

    rows_back, expert_weight_gradients = route_rows(grad_send, expert_back)
    expert_gate_weight_gradient, expert_up_weight_gradient, expert_down_weight_gradient = (
        expert_weight_gradients
    )
    back_flat = rows_back.reshape(local_experts * dp_count * slot_count, rows_back.shape[-1])
    mlp_partial = mlp_partial + jnp.sum(
        kept_state.slot_mask[:, :, None] * back_flat[kept_state.flat_index], axis=1
    )
    mlp_grad = lax.psum_scatter(mlp_partial, TENSOR, scatter_dimension=0, tiled=True)
    resid_from, mlpgain_part = rms_back(
        mlp_grad, kept_state.residual, kept_state.scale_two, mlp_gain
    )
    resid_grad = cotangent.astype(jnp.float32) + resid_from
    attn_rows = lax.all_gather(bfloat(resid_grad), TENSOR, axis=0, tiled=True)
    output_wgrad = first_dot(kept_state.attended_low, attn_rows)
    local_heads = kept_state.query_all.shape[1]
    attended_grad = bfloat(last_dot(attn_rows, kept_state.output_full)).reshape(
        group_rows, local_heads, VDIM
    )
    query_g, key_g, value_g = attend_back(
        kept_state.query_all,
        kept_state.key_all,
        kept_state.value_all,
        kept_state.doc_ids,
        (NOPE + ROPE) ** (-0.5),
        kept_state.log_total,
        attended_grad,
    )
    query_low = bfloat(query_g)
    key_low = bfloat(key_g)
    value_low = bfloat(value_g)
    query_unrot = rotate(
        query_low[..., NOPE:].astype(jnp.float32),
        kept_state.cos_group[:, None, :],
        -kept_state.sin_group[:, None, :],
    )
    qraw_grad = bfloat(
        jnp.concatenate([query_low[..., :NOPE].astype(jnp.float32), query_unrot], axis=-1)
    )
    qraw_grad = qraw_grad.reshape(group_rows, local_heads * (NOPE + ROPE))
    query_wgrad = first_dot(kept_state.normed_group, qraw_grad)
    normed_partial = last_dot(qraw_grad, kept_state.query_full)
    expand_rows = jnp.concatenate([key_low[..., :NOPE], value_low], axis=-1).reshape(
        group_rows, local_heads * (NOPE + VDIM)
    )
    expand_wgrad = first_dot(kept_state.latent_group, expand_rows)
    latent_partial = last_dot(expand_rows, kept_state.expand_full)
    keyrot_partial = jnp.sum(key_low[..., NOPE:].astype(jnp.float32), axis=1)
    normed_back, latent_back, keyrot_back = (
        lax.psum_scatter(
            normed_partial.astype(jnp.bfloat16), TENSOR, scatter_dimension=0, tiled=True
        ).astype(jnp.float32),
        lax.psum_scatter(
            latent_partial.astype(jnp.bfloat16), TENSOR, scatter_dimension=0, tiled=True
        ).astype(jnp.float32),
        lax.psum_scatter(
            keyrot_partial.astype(jnp.bfloat16), TENSOR, scatter_dimension=0, tiled=True
        ).astype(jnp.float32),
    )
    keyraw_back = rotate(keyrot_back, kept_state.cos_local, -kept_state.sin_local)
    latent_in, latgain_part = rms_back(
        latent_back, kept_state.latent_part, kept_state.scale_latent, latent_gain
    )
    latent_low = bfloat(jnp.concatenate([latent_in, keyraw_back], axis=-1))
    latent_wgrad = first_dot(kept_state.normed_one, latent_low)
    normed_total = normed_back + last_dot(latent_low, latent_weight)
    hidden_back, attngain_part = rms_back(
        normed_total, kept_state.hidden_f, kept_state.scale_one, attn_gain
    )
    hidden_grad = resid_grad + hidden_back
    fsdp_sums = (
        lax.psum_scatter(
            query_wgrad.astype(jnp.bfloat16), DP, scatter_dimension=0, tiled=True
        ).astype(jnp.float32),
        lax.psum_scatter(
            expand_wgrad.astype(jnp.bfloat16), DP, scatter_dimension=0, tiled=True
        ).astype(jnp.float32),
        lax.psum_scatter(
            output_wgrad.astype(jnp.bfloat16), DP, scatter_dimension=1, tiled=True
        ).astype(jnp.float32),
        lax.psum_scatter(
            sgate_wgrad.astype(jnp.bfloat16), DP, scatter_dimension=0, tiled=True
        ).astype(jnp.float32),
        lax.psum_scatter(
            sup_wgrad.astype(jnp.bfloat16), DP, scatter_dimension=0, tiled=True
        ).astype(jnp.float32),
        lax.psum_scatter(
            sdown_wgrad.astype(jnp.bfloat16), DP, scatter_dimension=1, tiled=True
        ).astype(jnp.float32),
    )
    small_sums = lax.psum(
        (latent_wgrad, attngain_part, mlpgain_part, latgain_part), (DP, TENSOR)
    )
    return (
        kept_state.layer_out,
        hidden_grad,
        small_sums[1],
        fsdp_sums[0],
        small_sums[0],
        small_sums[3],
        fsdp_sums[1],
        fsdp_sums[2],
        small_sums[2],
        fsdp_sums[3],
        fsdp_sums[4],
        fsdp_sums[5],
        expert_gate_weight_gradient,
        expert_up_weight_gradient,
        expert_down_weight_gradient,
    )


MESH = pl.DeviceIdType.MESH


def flip(index, bit):
    return index + bit - 2 * bit * ((index // bit) % 2)


def remote(src, dst, send_sem, recv_sem, peer):
    return pltpu.make_async_remote_copy(
        src_ref=src,
        dst_ref=dst,
        send_sem=send_sem,
        recv_sem=recv_sem,
        device_id=peer,
        device_id_type=MESH,
    )


def greet(peers):
    barrier = pltpu.get_barrier_semaphore()
    for peer in peers:
        pl.semaphore_signal(barrier, inc=1, device_id=peer, device_id_type=MESH)
    pl.semaphore_wait(barrier, len(peers))


def add_rows(target, size, *terms, store=None):
    step = 16
    while step * target.shape[1] < 65536 and size % (2 * step) == 0:
        step *= 2

    def one(i, carry):
        at = pl.ds(pl.multiple_of(i * step, step), step)
        total = target[at, :].astype(jnp.float32)
        for term in terms:
            total = total + term[at, :].astype(jnp.float32)
        to = target if store is None else store
        to[at, :] = total.astype(to.dtype)
        return carry

    lax.fori_loop(0, size // step, one, 0)


def sum_copies(blocks, core_buf, far_buf, x_buf, y_buf, sends, recvs, by_core, by_x, by_y):
    half = blocks.shape[2] // 2
    first, last = pl.ds(0, half), pl.ds(half, half)

    def copy(kind, j):
        at = blocks.at[lax.rem(j, 2)].at
        n, src, dst, peer = {
            K_CORE_OWN: lambda: (0, at[1], core_buf.at[j, 0], by_core),
            K_CORE_X: lambda: (1, at[4], core_buf.at[j, 1], by_core),
            K_CORE_Y: lambda: (2, at[5], core_buf.at[j, 2], by_core),
            K_CORE_FAR: lambda: (3, at[7], core_buf.at[j, 3], by_core),
            K_FAR_X: lambda: (4, at[6, first], far_buf.at[j, 0], by_x),
            K_FAR_Y: lambda: (5, at[6, last], far_buf.at[j, 1], by_y),
            K_X_FIRST: lambda: (6, at[2, first], x_buf.at[j, 0], by_x),
            K_X_LAST: lambda: (7, at[2, last], x_buf.at[j, 1], by_x),
            K_Y_FIRST: lambda: (8, at[3, first], y_buf.at[j, 0], by_y),
            K_Y_LAST: lambda: (9, at[3, last], y_buf.at[j, 1], by_y),
        }[kind]()
        return remote(src, dst, sends.at[n, j], recvs.at[n, j], peer)

    return copy


SUM_KINDS = (
    K_CORE_OWN,
    K_CORE_X,
    K_CORE_Y,
    K_CORE_FAR,
    K_FAR_X,
    K_FAR_Y,
    K_X_FIRST,
    K_X_LAST,
    K_Y_FIRST,
    K_Y_LAST,
)


SLOTS = (0, 1, 2, 4, 3, 5, 6, 7)


def moe_kernel(
    rows,
    back,
    gates,
    expert_gate,
    expert_up,
    shared_all,
    residual,
    cotangent,
    gain,
    rows_all,
    act_all,
    gpre_all,
    upre_all,
    resid_grad,
    resid_low,
    gain_grad,
    grad_out,
    gate_rows,
    up_rows,
    row_buf,
    back_buf,
    out_buf,
    blocks,
    core_buf,
    far_buf,
    x_buf,
    y_buf,
    ring_buf,
    ring_out,
    weight_sem,
    load_sem,
    back_sem,
    store_sem,
    ag_send,
    ag_recv,
    rs_send,
    rs_recv,
    ring_send,
    ring_recv,
    *,
    expert_width,
    routed_width,
):
    me, rank = lax.axis_index(DP), lax.axis_index(TENSOR)
    ranks = lax.axis_size(TENSOR)
    right = (me, lax.rem(rank + 1, ranks))
    left = (me, lax.rem(rank + ranks - 1, ranks))
    by_core, by_x, by_y = [(flip(me, bit), rank) for bit in (1, 2, 4)]
    count = rows.shape[0]
    half = count // 2
    first, last = pl.ds(0, half), pl.ds(half, half)
    hidden_width = gate_rows.shape[0]
    shared_pad = shared_all.shape[1]
    greet([by_core, by_x, by_y, right, left])

    def ag(kind, j, src, dst, peer):
        return remote(src, dst, ag_send.at[kind, j], ag_recv.at[kind, j], peer)

    def rs(kind, j, src, dst, peer):
        return remote(src, dst, rs_send.at[kind, j], rs_recv.at[kind, j], peer)

    def row_copy(kind, j):
        at = rows_all.at
        return {
            K_RING: lambda: ag(0, j, at[0, j - 1], at[0, j], right),
            K_X: lambda: ag(1, j, at[0, j], at[2, j], by_x),
            K_Y: lambda: ag(2, j, at[0, j], at[3, j], by_y),
            K_CORE: lambda: ag(3, j, at[0, j], at[1, j], by_core),
            K_FAR_Y: lambda: ag(4, j, at[2, j, last], at[6, j, last], by_y),
            K_FAR_X: lambda: ag(5, j, at[3, j, first], at[6, j, first], by_x),
            K_CORE_X: lambda: ag(6, j, at[2, j], at[4, j], by_core),
            K_CORE_Y: lambda: ag(7, j, at[3, j], at[5, j], by_core),
            K_CORE_FAR: lambda: ag(8, j, at[6, j], at[7, j], by_core),
            K_FAR_RING: lambda: ag(4, j, at[6, j - 1], at[6, j], right),
        }[kind]()

    def sum_copy(kind, j):
        at = blocks.at[lax.rem(j, 2)].at
        return {
            K_CORE_OWN: lambda: rs(0, j, at[1], core_buf.at[j, 0], by_core),
            K_CORE_X: lambda: rs(1, j, at[4], core_buf.at[j, 1], by_core),
            K_CORE_Y: lambda: rs(2, j, at[5], core_buf.at[j, 2], by_core),
            K_CORE_FAR: lambda: rs(3, j, at[7], core_buf.at[j, 3], by_core),
            K_FAR_X: lambda: rs(4, j, at[6, first], far_buf.at[j, 0], by_x),
            K_FAR_Y: lambda: rs(5, j, at[6, last], far_buf.at[j, 1], by_y),
            K_X_FIRST: lambda: rs(6, j, at[2, first], x_buf.at[j, 0], by_x),
            K_X_LAST: lambda: rs(7, j, at[2, last], x_buf.at[j, 1], by_x),
            K_Y_FIRST: lambda: rs(8, j, at[3, first], y_buf.at[j, 0], by_y),
            K_Y_LAST: lambda: rs(9, j, at[3, last], y_buf.at[j, 1], by_y),
        }[kind]()

    def ring_copy(step):
        return remote(
            ring_out.at[step], ring_buf.at[step], ring_send.at[step], ring_recv.at[step], right
        )

    def back_load(j, p, parity):
        return pltpu.make_async_copy(
            back.at[pl.ds(2 * p, 2), j], back_buf.at[parity], back_sem.at[parity]
        )

    def row_load(j, p, parity):
        return pltpu.make_async_copy(
            rows_all.at[pl.ds(2 * p, 2), j], row_buf.at[parity], load_sem.at[parity]
        )

    def stores(j, p, parity):
        return [
            pltpu.make_async_copy(
                out_buf.at[parity, n], to.at[pl.ds(2 * p, 2), j], store_sem.at[parity, n]
            )
            for n, to in enumerate((act_all, gpre_all, upre_all))
        ]

    def compute(j, p, place, following, used):
        parity = place % 2
        if following is not None:
            back_load(*following, 1 - parity).start()
        back_load(j, p, parity).wait()
        for copy in stores(*used, parity) if used is not None else ():
            copy.wait()
        row_load(j, p, parity).wait()
        wide = row_buf[parity].reshape(2 * count, row_buf.shape[3])
        gate_pre = last_dot(wide, gate_rows[...])
        up_pre = last_dot(wide, up_rows[...])
        column = lax.broadcasted_iota(jnp.int32, (1, hidden_width), 1)
        lanes = pl.ds(pl.multiple_of(j * count, count), count)
        gate = jnp.concatenate([gates[2 * p + i, :, lanes].T for i in range(2)], axis=0)
        scaled = jnp.where(
            column < expert_width,
            gate[:, 0:1],
            jnp.where(column < routed_width, gate[:, 1:2], 1.0),
        )
        sigmoid = 1.0 / (1.0 + jnp.exp(-gate_pre))
        silu = gate_pre * sigmoid
        dsilu = sigmoid * (1.0 + gate_pre * (1.0 - sigmoid))
        back_pre = back_buf[parity].reshape(2 * count, hidden_width).astype(jnp.float32) * scaled
        act = bfloat(silu * up_pre * scaled)
        gate_grad = bfloat(back_pre * up_pre * dsilu)
        up_grad = bfloat(back_pre * silu)
        out_buf[parity, 0] = act.reshape(2, count, hidden_width)
        out_buf[parity, 1] = gate_grad.reshape(2, count, hidden_width)
        out_buf[parity, 2] = up_grad.reshape(2, count, hidden_width)
        for copy in stores(j, p, parity):
            copy.start()
        grad = plain_dot(gate_grad, gate_rows[...]) + plain_dot(up_grad, up_rows[...])
        blocks[lax.rem(j, 2), pl.ds(2 * p, 2)] = bfloat(grad).reshape(2, count, grad.shape[1])

    own = pltpu.make_async_copy(rows, rows_all.at[0, 0], load_sem.at[0])
    own.start()
    assembled = []
    for n, (routed, target) in enumerate(((expert_gate, gate_rows), (expert_up, up_rows))):
        for i, (src, at) in enumerate(
            ((routed, pl.ds(0, routed_width)), (shared_all.at[n], pl.ds(routed_width, shared_pad)))
        ):
            copy = pltpu.make_async_copy(src, target.at[at], weight_sem.at[n, i])
            copy.start()
            assembled.append(copy)
        target[routed_width + shared_pad :] = jnp.zeros(
            (hidden_width - routed_width - shared_pad, target.shape[1]), jnp.bfloat16
        )
    back_load(0, 0, 0).start()
    own.wait()
    ring0 = row_copy(K_RING, 1)
    ring0.start()
    for kind in (K_X, K_Y, K_CORE):
        row_copy(kind, 0).start()
    for copy in assembled:
        copy.wait()

    def send_piece(j):
        for kind in (K_X, K_Y, K_CORE):
            row_copy(kind, j).start()

    def forward_piece(j):
        row_copy(K_X, j).wait_recv()
        row_copy(K_CORE_X, j).start()
        row_copy(K_Y, j).wait_recv()
        row_copy(K_CORE_Y, j).start()

    def sums_far(j):
        sum_copy(K_CORE_FAR, j).wait_recv()
        add_rows(blocks.at[lax.rem(j, 2), 6], count, core_buf.at[j, 3])
        sum_copy(K_FAR_X, j).start()
        sum_copy(K_FAR_Y, j).start()

    def sums_near(j):
        at = blocks.at[lax.rem(j, 2)].at
        sum_copy(K_CORE_X, j).wait_recv()
        add_rows(at[2, first], half, core_buf.at[j, 1, first])
        sum_copy(K_X_FIRST, j).start()
        sum_copy(K_CORE_Y, j).wait_recv()
        add_rows(at[3, last], half, core_buf.at[j, 2, last])
        sum_copy(K_Y_LAST, j).start()

    def sums_next(j):
        at = blocks.at[lax.rem(j, 2)].at
        sum_copy(K_FAR_X, j).wait_recv()
        add_rows(at[3, first], half, core_buf.at[j, 2, first], far_buf.at[j, 0])
        sum_copy(K_Y_FIRST, j).start()
        sum_copy(K_FAR_Y, j).wait_recv()
        add_rows(at[2, last], half, core_buf.at[j, 1, last], far_buf.at[j, 1])
        sum_copy(K_X_LAST, j).start()

    def sums_last(j):
        at = blocks.at[lax.rem(j, 2)].at
        for kind in (K_CORE_OWN, K_X_FIRST, K_X_LAST, K_Y_FIRST, K_Y_LAST):
            sum_copy(kind, j).wait_recv()
        terms = [
            (core_buf.at[j, 0, part], x_buf.at[j, n], y_buf.at[j, n])
            for n, part in enumerate((first, last))
        ]

        @pl.when(j == 0)
        def _():
            for part, more in zip((first, last), terms):
                add_rows(at[0, part], half, *more, store=grad_out.at[part])

        @pl.when(j == 1)
        def _():
            for part, more in zip((first, last), terms):
                add_rows(at[0, part], half, *more, store=ring_out.at[0, part])
            ring_copy(0).start()

        @pl.when(j > 1)
        def _():
            ring_copy(j - 2).wait_recv()
            for part, more in zip((first, last), terms):
                add_rows(
                    at[0, part],
                    half,
                    *more,
                    ring_buf.at[j - 2, part],
                    store=ring_out.at[j - 1, part],
                )
            ring_copy(j - 1).start()

        for kind in SUM_KINDS:
            sum_copy(kind, j).wait_send()

    row_copy(K_CORE, 0).wait_recv()
    row_load(0, 0, 0).start()
    compute(0, 0, 0, (0, 1), None)
    sum_copy(K_CORE_OWN, 0).start()
    row_copy(K_RING, 1).wait_recv()
    row_copy(K_RING, 2).start()
    send_piece(1)
    row_copy(K_X, 0).wait_recv()
    row_copy(K_FAR_Y, 0).start()
    row_copy(K_CORE_X, 0).start()
    row_copy(K_Y, 0).wait_recv()
    row_copy(K_FAR_X, 0).start()
    row_copy(K_CORE_Y, 0).start()
    row_load(0, 1, 1).start()
    compute(0, 1, 1, (0, 2), None)
    row_copy(K_RING, 2).wait_recv()
    row_copy(K_RING, 3).start()
    send_piece(2)
    row_copy(K_CORE_X, 0).wait_recv()
    row_copy(K_CORE_Y, 0).wait_recv()
    row_load(0, 2, 0).start()
    row_copy(K_FAR_X, 0).wait_recv()
    row_copy(K_FAR_Y, 0).wait_recv()
    row_copy(K_CORE_FAR, 0).start()
    row_copy(K_FAR_RING, 1).start()
    compute(0, 2, 0, (0, 3), (0, 0))
    sum_copy(K_CORE_X, 0).start()
    sum_copy(K_CORE_Y, 0).start()
    row_copy(K_CORE_FAR, 0).wait_recv()
    row_load(0, 3, 1).start()
    row_copy(K_RING, 3).wait_recv()
    send_piece(3)
    forward_piece(1)
    row_copy(K_CORE, 1).wait_recv()
    compute(0, 3, 1, (1, 3), (0, 1))
    sum_copy(K_CORE_FAR, 0).start()
    sums_near(0)
    sums_far(0)
    row_copy(K_FAR_RING, 1).wait_recv()
    row_copy(K_CORE_FAR, 1).start()
    row_copy(K_FAR_RING, 2).start()
    row_copy(K_CORE_FAR, 1).wait_recv()
    row_load(1, 3, 0).start()

    def body(j, carry):
        before = j - 1
        row_copy(K_CORE_X, j).wait_recv()
        row_copy(K_CORE_Y, j).wait_recv()
        row_load(j, 2, 1).start()

        @pl.when(j == 1)
        def _():
            for copy in stores(0, 2, 0):
                copy.wait()

        @pl.when(j > 1)
        def _():
            for copy in stores(before, 1, 0):
                copy.wait()

        compute(j, 3, 0, (j, 2), None)
        sum_copy(K_CORE_FAR, j).start()

        @pl.when(j == 1)
        def _():
            sums_next(0)
            for copy in stores(0, 3, 1):
                copy.wait()

        @pl.when(j > 1)
        def _():
            for copy in stores(before, 0, 1):
                copy.wait()

        row_load(j, 1, 0).start()
        compute(j, 2, 1, (j, 1), None)
        sum_copy(K_CORE_X, j).start()
        sum_copy(K_CORE_Y, j).start()
        sums_far(j)

        @pl.when(j < ranks - 1)
        def _():
            row_copy(K_FAR_RING, j + 1).wait_recv()
            row_copy(K_CORE_FAR, j + 1).start()

            @pl.when(j < ranks - 2)
            def _():
                row_copy(K_FAR_RING, j + 2).start()

        row_load(j, 0, 1).start()
        compute(j, 1, 0, (j, 0), (j, 3))
        sums_near(j)

        @pl.when(j < ranks - 1)
        def _():
            forward_piece(j + 1)
            row_copy(K_CORE, j + 1).wait_recv()
            row_copy(K_CORE_FAR, j + 1).wait_recv()
            row_load(j + 1, 3, 0).start()
            back_load(j + 1, 3, 0).start()

        compute(j, 0, 1, None, (j, 2))
        sum_copy(K_CORE_OWN, j).start()
        sums_last(before)
        sums_next(j)
        return carry

    lax.fori_loop(1, ranks, body, 0)
    sums_last(ranks - 1)
    ring_copy(ranks - 2).wait_recv()
    grad = grad_out[...] + ring_buf[ranks - 2].astype(jnp.float32)
    values = residual[...]
    scale = lax.rsqrt(jnp.mean(values * values, axis=-1, keepdims=True) + epsilon)
    scaled_grad = grad * gain[...]
    inner = jnp.mean(scaled_grad * values, axis=-1, keepdims=True)
    through = scale * scaled_grad - values * (scale * scale * scale) * inner
    total = cotangent[...].astype(jnp.float32) + through
    resid_grad[...] = total
    resid_low[...] = bfloat(total)
    gain_grad[...] = jnp.sum(grad * values * scale, axis=0, keepdims=True)
    for step in range(ranks - 1):
        ring_copy(step).wait_send()
        row_copy(K_RING, step + 1).wait_send()
    for p in (1, 0):
        for copy in stores(ranks - 1, p, 1 - p):
            copy.wait()

    def drain(j, carry):
        for kind in (K_X, K_Y, K_CORE, K_CORE_X, K_CORE_Y, K_CORE_FAR):
            row_copy(kind, j).wait_send()
        return carry

    row_copy(K_FAR_X, 0).wait_send()
    row_copy(K_FAR_Y, 0).wait_send()
    for j in range(1, ranks):
        row_copy(K_FAR_RING, j).wait_send()
    lax.fori_loop(0, ranks, drain, 0)


def moe_pass(
    rows,
    back,
    gates,
    expert_gate,
    expert_up,
    shared_all,
    residual,
    cotangent,
    gain,
    expert_width,
):
    ranks = lax.axis_size(TENSOR)
    groups = lax.axis_size(DP)
    count, width = rows.shape
    hidden_width = back.shape[-1]
    anywhere = pl.BlockSpec(memory_space=pl.ANY)
    in_vmem = pl.BlockSpec(memory_space=pltpu.VMEM)
    low = jnp.bfloat16
    hidden_shape = jax.ShapeDtypeStruct((groups, ranks, count, hidden_width), low)
    dma = pltpu.SemaphoreType.DMA
    return pl.pallas_call(
        functools.partial(
            moe_kernel, expert_width=expert_width, routed_width=expert_gate.shape[0]
        ),
        out_shape=(
            jax.ShapeDtypeStruct((groups, ranks, count, width), low),
            hidden_shape,
            hidden_shape,
            hidden_shape,
            jax.ShapeDtypeStruct((count, width), jnp.float32),
            jax.ShapeDtypeStruct((count, width), low),
            jax.ShapeDtypeStruct((1, width), jnp.float32),
        ),
        in_specs=[anywhere, anywhere, in_vmem] + [anywhere] * 3 + [in_vmem] * 3,
        out_specs=(anywhere,) * 4 + (in_vmem,) * 3,
        scratch_shapes=[
            pltpu.VMEM((count, width), jnp.float32),
            pltpu.VMEM((hidden_width, width), low),
            pltpu.VMEM((hidden_width, width), low),
            pltpu.VMEM((2, 2, count, width), low),
            pltpu.VMEM((2, 2, count, hidden_width), low),
            pltpu.VMEM((2, 3, 2, count, hidden_width), low),
            pltpu.VMEM((2, groups, count, width), low),
            pltpu.VMEM((ranks, 4, count, width), low),
            pltpu.VMEM((ranks, 2, count // 2, width), low),
            pltpu.VMEM((ranks, 2, count // 2, width), low),
            pltpu.VMEM((ranks, 2, count // 2, width), low),
            pltpu.VMEM((ranks - 1, count, width), low),
            pltpu.VMEM((ranks - 1, count, width), low),
            dma((2, 2)),
            dma((2,)),
            dma((2,)),
            dma((2, 3)),
            dma((9, ranks)),
            dma((9, ranks)),
            dma((10, ranks)),
            dma((10, ranks)),
            dma((ranks - 1,)),
            dma((ranks - 1,)),
        ],
        compiler_params=pltpu.CompilerParams(
            collective_id=2, has_side_effects=True, vmem_limit_bytes=60 * 1024 * 1024
        ),
        name="moe_pass",
    )(
        rows,
        back,
        gates,
        expert_gate,
        expert_up,
        shared_all,
        residual,
        cotangent,
        gain,
    )


def cube_copies(gathered, sends, recvs, by_core, by_x, by_y):
    half = gathered.shape[2] // 2
    first, last = pl.ds(0, half), pl.ds(half, half)
    at = gathered.at

    def copy(kind, j):
        src, dst, peer = {
            K_X: lambda: (at[0, j], at[2, j], by_x),
            K_Y: lambda: (at[0, j], at[3, j], by_y),
            K_CORE: lambda: (at[0, j], at[1, j], by_core),
            K_FAR_Y: lambda: (at[2, j, last], at[6, j, last], by_y),
            K_FAR_X: lambda: (at[3, j, first], at[6, j, first], by_x),
            K_CORE_X: lambda: (at[2, j], at[4, j], by_core),
            K_CORE_Y: lambda: (at[3, j], at[5, j], by_core),
            K_CORE_FAR: lambda: (at[6, j], at[7, j], by_core),
        }[kind]()
        return remote(src, dst, sends.at[kind, j], recvs.at[kind, j], peer)

    return copy


def swap_halves(values):
    lane = lax.broadcasted_iota(jnp.int32, values.shape, 1)
    middle = ROPE // 2
    lanes = values.shape[1]
    ahead, behind = pltpu.roll(values, lanes - middle, 1), pltpu.roll(values, middle, 1)
    return jnp.where((lane // middle) % 2 == 0, ahead, behind)


def turn(values, cos_table, sin_table):
    return values * cos_table + swap_halves(values) * sin_table


def front_kernel(
    lengths,
    hidden,
    cotangent,
    query,
    expand,
    output,
    shared,
    expert_down,
    routes,
    route_gates,
    latent_rows,
    attn_gain,
    latent_gain,
    mlp_gain,
    frequency,
    normed_out,
    latent_out,
    own_latent,
    query_out,
    expand_out,
    output_out,
    qcat_out,
    kcat_out,
    value_out,
    prob_out,
    attended_out,
    cos_out,
    sin_out,
    residual_out,
    normed_two,
    shared_all,
    gates_all,
    cotan_all,
    back_all,
    hidden_all,
    query_all,
    expand_all,
    output_all,
    down_rows,
    normed,
    latent_low,
    q_cat,
    k_cat,
    value,
    mask,
    prob,
    attended,
    gate_abs,
    gate_rel,
    gate_send,
    row_buf,
    back_buf,
    ring_out,
    ring_buf,
    local_sem,
    prob_sem,
    row_sem,
    back_sem,
    ring_send,
    ring_recv,
    w_send,
    w_recv,
    deal_send,
    deal_recv,
    gates_send,
    gates_recv,
    cring_send,
    cring_recv,
    c_send,
    c_recv,
    sum_send,
    sum_recv,
):
    me, rank = lax.axis_index(DP), lax.axis_index(TENSOR)
    ranks, count = lax.axis_size(TENSOR), lax.axis_size(DP)
    right = (me, lax.rem(rank + 1, ranks))
    left = (me, lax.rem(rank + ranks - 1, ranks))
    by_core, by_x, by_y = [(flip(me, bit), rank) for bit in (1, 2, 4)]
    partners = []
    for k in range(1, count):
        other = me
        for bit in (1, 2, 4):
            other = flip(other, bit) if k & bit else other
        partners.append((k, (other, rank)))
    rows, width = hidden.shape
    group_rows = rows * ranks
    heads = q_cat.shape[0]
    local_experts = gate_abs.shape[0] // count
    q_rows, e_rows, o_cols = query.shape[0], expand.shape[0], output.shape[1]
    routed_width = expert_down.shape[0]
    shared_pad = shared.shape[2]
    piece = shared.shape[3]

    def query_at(owner, half=None):
        size = q_rows if half is None else q_rows // 2
        start = owner * q_rows + (0 if half is None else half * size)
        return query_all.at[pl.ds(pl.multiple_of(start, size), size)]

    def expand_at(owner, half=None):
        size = e_rows if half is None else e_rows // 2
        start = owner * e_rows + (0 if half is None else half * size)
        return expand_all.at[pl.ds(pl.multiple_of(start, size), size)]

    def output_at(owner, half=None):
        size = output.shape[0] if half is None else output.shape[0] // 2
        start = 0 if half is None else half * size
        return output_all.at[
            pl.ds(start, size), pl.ds(pl.multiple_of(owner * o_cols, o_cols), o_cols)
        ]

    greet([peer for _, peer in partners] + [right, left])

    ring = {}

    def ring_step(step):
        src = hidden if step == 0 else hidden_all.at[step]
        ring[step] = remote(
            src, hidden_all.at[step + 1], ring_send.at[step], ring_recv.at[step], right
        )
        ring[step].start()

    weights = ((query, query_at), (expand, expand_at), (output, output_at))
    copies = {}

    def send(i, kind, src, dst, peer):
        copies[i, kind] = remote(src, dst, w_send.at[i, kind], w_recv.at[i, kind], peer)
        copies[i, kind].start()

    def weight_first(i):
        own, at = weights[i]
        send(i, 0, own, at(me), by_x)
        send(i, 1, own, at(me), by_y)
        send(i, 2, own, at(me), by_core)

    def weight_forward(i):
        _, at = weights[i]
        copies[i, 0].wait_recv()
        send(i, 3, at(flip(me, 2), 1), at(flip(me, 2), 1), by_y)
        send(i, 4, at(flip(me, 2)), at(flip(me, 2)), by_core)
        copies[i, 1].wait_recv()
        send(i, 5, at(flip(me, 4), 0), at(flip(me, 4), 0), by_x)
        send(i, 6, at(flip(me, 4)), at(flip(me, 4)), by_core)

    def weight_far(i):
        _, at = weights[i]
        far = flip(flip(me, 2), 4)
        copies[i, 3].wait_recv()
        copies[i, 5].wait_recv()
        send(i, 7, at(far), at(far), by_core)

    def weight_last(i):
        for kind in (2, 4, 6, 7):
            copies[i, kind].wait_recv()

    cube = cube_copies(cotan_all, c_send, c_recv, by_core, by_x, by_y)

    def cotan_ring(j):
        src = cotan_all.at[0, j - 1]
        return remote(src, cotan_all.at[0, j], cring_send.at[j - 1], cring_recv.at[j - 1], right)

    def cotan_send(j):
        for kind in (K_X, K_Y, K_CORE):
            cube(kind, j).start()

    def cotan_forward(j):
        cube(K_X, j).wait_recv()
        cube(K_FAR_Y, j).start()
        cube(K_CORE_X, j).start()
        cube(K_Y, j).wait_recv()
        cube(K_FAR_X, j).start()
        cube(K_CORE_Y, j).start()

    def cotan_far(j):
        cube(K_FAR_X, j).wait_recv()
        cube(K_FAR_Y, j).wait_recv()
        cube(K_CORE_FAR, j).start()

    def cotan_next(j):
        cotan_ring(j).wait_recv()
        if j + 1 < ranks:
            cotan_ring(j + 1).start()
        cotan_send(j)

    def down_back(j, begin=0, end=4):
        needs = ((K_CORE,), (), (K_CORE_X, K_CORE_Y), (K_CORE_FAR,))
        for p in range(begin, end):
            for kind in needs[p]:
                cube(kind, j).wait_recv()

        def load(p, parity):
            return pltpu.make_async_copy(
                cotan_all.at[pl.ds(2 * p, 2), j], row_buf.at[parity], row_sem.at[parity]
            )

        def store(p, parity):
            return pltpu.make_async_copy(
                back_buf.at[parity], back_all.at[pl.ds(2 * p, 2), j], back_sem.at[parity]
            )

        load(begin, begin % 2).start()

        def one(p, carry):
            parity = lax.rem(p, 2)
            load(p, parity).wait()

            @pl.when(p + 1 < end)
            def _():
                load(p + 1, 1 - parity).start()

            @pl.when(p > begin + 1)
            def _():
                store(p - 2, parity).wait()

            wide = row_buf[parity].reshape(2 * rows, width)
            back = bfloat(last_dot(wide, down_rows[...]))
            back_buf[parity] = back.reshape(2, rows, back.shape[1])
            store(p, parity).start()
            return carry

        lax.fori_loop(begin, end, one, 0)
        for p in range(max(begin, end - 2), end):
            store(p, p % 2).wait()

    ring_step(0)
    weight_first(0)
    weight_first(1)
    dealt = []
    for n, (k, peer) in enumerate(partners):
        copy = remote(
            shared.at[peer[0]],
            shared_all.at[:, :, pl.ds(pl.multiple_of(me * piece, piece), piece)],
            deal_send.at[n],
            deal_recv.at[n],
            peer,
        )
        dealt.append(copy)
    local = [
        pltpu.make_async_copy(hidden, hidden_all.at[0], local_sem.at[0]),
        pltpu.make_async_copy(query, query_at(me), local_sem.at[1]),
        pltpu.make_async_copy(expand, expand_at(me), local_sem.at[2]),
        pltpu.make_async_copy(output, output_at(me), local_sem.at[3]),
        pltpu.make_async_copy(
            shared.at[me],
            shared_all.at[:, :, pl.ds(pl.multiple_of(me * piece, piece), piece)],
            local_sem.at[4],
        ),
        pltpu.make_async_copy(cotangent, cotan_all.at[0, 0], local_sem.at[5]),
        pltpu.make_async_copy(expert_down, down_rows.at[pl.ds(0, routed_width)], local_sem.at[6]),
    ]
    for copy in local:
        copy.start()

    def absolute(index):
        block = index // rows
        return ((rank + ranks - block) % ranks) * rows + index % rows

    def starts_of(token):
        start, total = jnp.zeros_like(token), 0
        for n in range(lengths.shape[1]):
            total = total + lengths[0, n]
            start = jnp.where(token >= total, total, start)
        return start

    token = absolute(lax.broadcasted_iota(jnp.int32, (group_rows, cos_out.shape[1]), 0))
    angle = (token - starts_of(token)).astype(jnp.float32) * frequency[...]
    lane = lax.broadcasted_iota(jnp.int32, angle.shape, 1)
    cos_out[...] = jnp.cos(angle)
    sine = jnp.sin(angle)
    sin_out[...] = jnp.where((lane // (ROPE // 2)) % 2 == 0, -sine, sine)
    row_token = absolute(lax.broadcasted_iota(jnp.int32, mask.shape, 0))
    column_token = absolute(lax.broadcasted_iota(jnp.int32, mask.shape, 1))
    allowed = (column_token <= row_token) & (column_token >= starts_of(row_token))
    mask[...] = jnp.where(allowed, 0.0, -jnp.inf)

    expert = lax.broadcasted_iota(jnp.int32, gate_abs.shape, 0)
    dense = jnp.zeros(gate_abs.shape, jnp.float32)
    for k in range(routes.shape[0]):
        dense = dense + jnp.where(routes[k : k + 1, :] == expert, route_gates[k : k + 1, :], 0.0)
    gate_abs[...] = dense
    for r in range(ranks):
        start = pl.multiple_of(((rank + ranks - r) % ranks) * rows, rows)
        gate_rel[:, r * rows : (r + 1) * rows] = gate_abs[:, pl.ds(start, rows)]
    gate_send[...] = jnp.zeros_like(gate_send)
    for p in range(count):
        gate_send[p, 0:local_experts] = gate_rel[p * local_experts : (p + 1) * local_experts]
    down_rows[routed_width + shared_pad :] = jnp.zeros(
        (down_rows.shape[0] - routed_width - shared_pad, width), jnp.bfloat16
    )
    gate_copies = []
    for n, (k, peer) in enumerate(partners):
        gate_copies.append(
            remote(
                gate_send.at[peer[0]],
                gates_all.at[SLOTS.index(k)],
                gates_send.at[n],
                gates_recv.at[n],
                peer,
            )
        )
    own_gates = pltpu.make_async_copy(gate_send.at[me], gates_all.at[0], local_sem.at[7])
    own_gates.start()

    def norm_piece(r):
        at = pl.ds(r * rows, rows)
        values = hidden_all[r].astype(jnp.float32)
        scale = lax.rsqrt(jnp.mean(values * values, axis=-1, keepdims=True) + epsilon)
        normed[at, :] = bfloat(values * scale * attn_gain[...])

    def project_piece(r):
        at = pl.ds(r * rows, rows)
        values = normed[at, :]
        cos_table, sin_table = cos_out[at, :], sin_out[at, :]
        lanes = cos_table.shape[1]
        raw = plain_dot(values, query_all[...])
        for h in range(heads):
            q_cat[h, at, 0:NOPE] = bfloat(raw[:, h * NOPE : (h + 1) * NOPE])
        for pair in range(heads // 2):
            start = heads * NOPE + pair * lanes
            turned = bfloat(turn(raw[:, start : start + lanes], cos_table, sin_table))
            q_cat[2 * pair, at, NOPE : NOPE + lanes] = turned
            q_cat[2 * pair + 1, at, NOPE : NOPE + lanes] = turned
        latent = last_dot(values, latent_rows[...])
        part = latent[:, :LATENT]
        if r == 0:
            own_latent[...] = part
        scale = lax.rsqrt(jnp.mean(part * part, axis=-1, keepdims=True) + epsilon)
        low_part = bfloat(part * scale * latent_gain[...])
        latent_low[at, :] = low_part
        turned = turn(latent[:, LATENT:], cos_table, sin_table)
        lane = lax.broadcasted_iota(jnp.int32, turned.shape, 1)
        even = bfloat(jnp.where(lane < ROPE, turned, 0.0))
        odd = bfloat(jnp.where(lane < ROPE, 0.0, turned))
        expanded = plain_dot(low_part, expand_all[...])
        step = NOPE + VDIM
        for h in range(heads):
            k_cat[h, at, 0:NOPE] = bfloat(expanded[:, h * step : h * step + NOPE])
            k_cat[h, at, NOPE : NOPE + lanes] = even if h % 2 == 0 else odd
            value[h, at, :] = bfloat(expanded[:, h * step + NOPE : (h + 1) * step])

    def prob_store(h, parity):
        return pltpu.make_async_copy(prob.at[parity], prob_out.at[h], prob_sem.at[parity])

    def head(h):
        parity = h % 2
        if h >= 2:
            prob_store(h - 2, parity).wait()
        scores = last_dot(q_cat[h], k_cat[h]) * (NOPE + ROPE) ** (-0.5) + mask[...]
        exp_scores = jnp.exp(scores - jnp.max(scores, axis=-1, keepdims=True))
        ratio = exp_scores / jnp.sum(exp_scores, axis=-1, keepdims=True)
        prob[parity] = ratio
        prob_store(h, parity).start()
        attended[:, h * VDIM : (h + 1) * VDIM] = bfloat(plain_dot(bfloat(ratio), value[h]))

    norm_piece_wait = [local[0].wait] + [lambda s=s: ring[s].wait_recv() for s in range(ranks - 1)]
    norm_piece_wait[0]()
    norm_piece(0)
    weight_first(2)
    weight_forward(0)
    norm_piece_wait[1]()
    ring_step(1)
    weight_forward(1)
    norm_piece(1)
    weight_far(0)
    weight_far(1)
    local[5].wait()
    cotan_send(0)
    norm_piece_wait[2]()
    ring_step(2)
    cotan_ring(1).start()
    norm_piece(2)
    weight_forward(2)
    weight_last(0)
    weight_last(1)
    local[1].wait()
    local[2].wait()
    project_piece(0)
    project_piece(1)
    weight_far(2)
    project_piece(2)
    norm_piece_wait[3]()
    norm_piece(3)
    cotan_forward(0)
    for copy in gate_copies:
        copy.start()
    for copy in dealt:
        copy.start()
    project_piece(3)
    cotan_next(1)
    for h in range(heads):
        head(h)
    weight_last(2)
    local[3].wait()

    def attn_block(r):
        return plain_dot(attended[r * rows : (r + 1) * rows, :], output_all[...])

    def sum_step(step):
        return remote(
            ring_out.at[step], ring_buf.at[step], sum_send.at[step], sum_recv.at[step], right
        )

    ring_out[0] = bfloat(attn_block(1))
    sum_step(0).start()
    cotan_far(0)
    for copy in dealt:
        copy.wait_recv()
    local[4].wait()
    local[6].wait()
    shared_down = pltpu.make_async_copy(
        shared_all.at[2], down_rows.at[pl.ds(routed_width, shared_pad)], local_sem.at[8]
    )
    shared_down.start()
    shared_down.wait()
    down_back(0)
    cotan_next(2)
    sum_step(0).wait_recv()
    ring_out[1] = bfloat(attn_block(2) + ring_buf[0].astype(jnp.float32))
    sum_step(1).start()
    outs = [
        pltpu.make_async_copy(src, dst, local_sem.at[9 + n])
        for n, (src, dst) in enumerate(
            (
                (normed, normed_out),
                (latent_low, latent_out),
                (query_all, query_out),
                (expand_all, expand_out),
                (output_all, output_out),
                (q_cat, qcat_out),
                (k_cat, kcat_out),
                (value, value_out),
                (attended, attended_out),
            )
        )
    ]
    for copy in outs:
        copy.start()
    cotan_forward(1)
    cotan_far(1)
    cotan_next(3)
    sum_step(1).wait_recv()
    ring_out[2] = bfloat(attn_block(3) + ring_buf[1].astype(jnp.float32))
    sum_step(2).start()
    down_back(1)
    cotan_forward(2)
    cotan_far(2)
    cotan_forward(3)
    sum_step(2).wait_recv()
    residual = (
        hidden_all[0].astype(jnp.float32) + attn_block(0) + ring_buf[2].astype(jnp.float32)
    )
    residual_out[...] = residual
    scale = lax.rsqrt(jnp.mean(residual * residual, axis=-1, keepdims=True) + epsilon)
    normed_two[...] = bfloat(residual * scale * mlp_gain[...])
    down_back(2)
    cotan_far(3)
    down_back(3, 0, 3)
    down_back(3, 3, 4)

    for h in (heads - 2, heads - 1):
        prob_store(h, h % 2).wait()
    for copy in outs:
        copy.wait()
    own_gates.wait()
    for copy in gate_copies:
        copy.wait()
    for copy in dealt:
        copy.wait_send()
    for i in range(len(weights)):
        for kind in range(8):
            copies[i, kind].wait_send()
    for step in range(ranks - 1):
        ring[step].wait_send()
        cotan_ring(step + 1).wait_send()
        sum_step(step).wait_send()
    for j in range(ranks):
        for kind in (
            K_X,
            K_Y,
            K_CORE,
            K_FAR_Y,
            K_FAR_X,
            K_CORE_X,
            K_CORE_Y,
            K_CORE_FAR,
        ):
            cube(kind, j).wait_send()


def front_pass(
    lengths,
    hidden,
    cotangent,
    query,
    expand,
    output,
    shared,
    expert_down,
    routes,
    route_gates,
    latent_rows,
    attn_gain,
    latent_gain,
    mlp_gain,
    hidden_width,
    experts,
):
    count, ranks = lax.axis_size(DP), lax.axis_size(TENSOR)
    rows, width = hidden.shape
    group_rows = rows * ranks
    heads = query.shape[1] // (NOPE + ROPE)
    lanes = 2 * ROPE
    low, full = jnp.bfloat16, jnp.float32
    frequency = rope_base ** (-jnp.arange(ROPE // 2, dtype=full) * 2.0 / ROPE)
    frequency = jnp.tile(frequency, lanes // (ROPE // 2))[None, :]
    anywhere = pl.BlockSpec(memory_space=pl.ANY)
    in_vmem = pl.BlockSpec(memory_space=pltpu.VMEM)
    dma = pltpu.SemaphoreType.DMA
    by_slot = (count, ranks, rows)

    def array(*shape, dtype=low):
        return jax.ShapeDtypeStruct(shape, dtype)

    def full_query():
        return (count * query.shape[0], query.shape[1])

    def full_expand():
        return (count * expand.shape[0], expand.shape[1])

    def full_output():
        return (output.shape[0], count * output.shape[1])

    return pl.pallas_call(
        front_kernel,
        out_shape=(
            array(group_rows, width),
            array(group_rows, LATENT),
            array(rows, LATENT, dtype=full),
            array(*full_query()),
            array(*full_expand()),
            array(*full_output()),
            array(heads, group_rows, NOPE + lanes),
            array(heads, group_rows, NOPE + lanes),
            array(heads, group_rows, VDIM),
            array(heads, group_rows, group_rows, dtype=full),
            array(group_rows, heads * VDIM),
            array(group_rows, lanes, dtype=full),
            array(group_rows, lanes, dtype=full),
            array(rows, width, dtype=full),
            array(rows, width),
            array(*shared.shape[1:3], count * shared.shape[3]),
            array(count, 8, group_rows, dtype=full),
            array(*by_slot, width),
            array(*by_slot, hidden_width),
        ),
        in_specs=[pl.BlockSpec(memory_space=pltpu.SMEM)] + [anywhere] * 7 + [in_vmem] * 7,
        out_specs=(anywhere, anywhere, in_vmem)
        + (anywhere,) * 8
        + (in_vmem,) * 4
        + (anywhere,) * 4,
        scratch_shapes=[
            pltpu.VMEM((ranks, rows, width), low),
            pltpu.VMEM(full_query(), low),
            pltpu.VMEM(full_expand(), low),
            pltpu.VMEM(full_output(), low),
            pltpu.VMEM((hidden_width, width), low),
            pltpu.VMEM((group_rows, width), low),
            pltpu.VMEM((group_rows, LATENT), low),
            pltpu.VMEM((heads, group_rows, NOPE + lanes), low),
            pltpu.VMEM((heads, group_rows, NOPE + lanes), low),
            pltpu.VMEM((heads, group_rows, VDIM), low),
            pltpu.VMEM((group_rows, group_rows), full),
            pltpu.VMEM((2, group_rows, group_rows), full),
            pltpu.VMEM((group_rows, heads * VDIM), low),
            pltpu.VMEM((experts, group_rows), full),
            pltpu.VMEM((experts, group_rows), full),
            pltpu.VMEM((count, 8, group_rows), full),
            pltpu.VMEM((2, 2, rows, width), low),
            pltpu.VMEM((2, 2, rows, hidden_width), low),
            pltpu.VMEM((ranks - 1, rows, width), low),
            pltpu.VMEM((ranks - 1, rows, width), low),
            dma((18,)),
            dma((2,)),
            dma((2,)),
            dma((2,)),
            dma((ranks - 1,)),
            dma((ranks - 1,)),
            dma((3, 8)),
            dma((3, 8)),
            dma((count - 1,)),
            dma((count - 1,)),
            dma((count - 1,)),
            dma((count - 1,)),
            dma((ranks - 1,)),
            dma((ranks - 1,)),
            dma((9, ranks)),
            dma((9, ranks)),
            dma((ranks - 1,)),
            dma((ranks - 1,)),
        ],
        compiler_params=pltpu.CompilerParams(
            collective_id=1, has_side_effects=True, vmem_limit_bytes=60 * 1024 * 1024
        ),
        name="front_pass",
    )(
        lengths,
        hidden,
        cotangent,
        query,
        expand,
        output,
        shared,
        expert_down,
        routes,
        route_gates,
        latent_rows,
        attn_gain,
        latent_gain,
        mlp_gain,
        frequency,
    )


def back_kernel(
    resid,
    acts,
    expert_down,
    shared_all,
    output,
    query,
    expand,
    q_cat,
    k_cat,
    value,
    prob_all,
    cos_table,
    sin_table,
    gate_all,
    up_all,
    row_all,
    resid_all,
    moe_sums,
    gate_out,
    up_out,
    shared_rows,
    normed_back,
    latent_back,
    query_grad,
    expand_grad,
    down_rows,
    act_buf,
    resid_buf,
    attended_grad,
    prob,
    pair,
    key_rot,
    blocks,
    core_buf,
    far_buf,
    x_buf,
    y_buf,
    ring_out,
    ring_buf,
    left_buf,
    right_buf,
    acc,
    local_sem,
    act_sem,
    prob_sem,
    sums_sem,
    load_sem,
    acc_sem,
    resid_send,
    resid_recv,
    s_send,
    s_recv,
    ring_send,
    ring_recv,
):
    me, rank = lax.axis_index(DP), lax.axis_index(TENSOR)
    ranks = lax.axis_size(TENSOR)
    right = (me, lax.rem(rank + 1, ranks))
    left = (me, lax.rem(rank + ranks - 1, ranks))
    by_core, by_x, by_y = [(flip(me, bit), rank) for bit in (1, 2, 4)]
    rows, width = resid.shape
    half = rows // 2
    first, last = pl.ds(0, half), pl.ds(half, half)
    heads = q_cat.shape[0]
    lanes = cos_table.shape[1]
    routed_width, shared_pad = expert_down.shape[0], shared_all.shape[1]
    scaling = (NOPE + ROPE) ** (-0.5)
    greet([by_core, by_x, by_y, right, left])

    local = [
        pltpu.make_async_copy(resid, resid_buf.at[0], local_sem.at[0]),
        pltpu.make_async_copy(expert_down, down_rows.at[pl.ds(0, routed_width)], local_sem.at[1]),
        pltpu.make_async_copy(
            shared_all.at[2], down_rows.at[pl.ds(routed_width, shared_pad)], local_sem.at[2]
        ),
    ]

    def resid_step(step):
        src = resid if step == 0 else resid_buf.at[step]
        return remote(
            src, resid_buf.at[step + 1], resid_send.at[step], resid_recv.at[step], right
        )

    resid_step(0).start()
    for copy in local:
        copy.start()
    down_rows[routed_width + shared_pad :] = jnp.zeros(
        (down_rows.shape[0] - routed_width - shared_pad, width), jnp.bfloat16
    )
    key_rot[...] = jnp.zeros_like(key_rot)

    copy_of = sum_copies(
        blocks, core_buf, far_buf, x_buf, y_buf, s_send, s_recv, by_core, by_x, by_y
    )

    def act_load(j, p, parity):
        return pltpu.make_async_copy(
            acts.at[pl.ds(2 * p, 2), j], act_buf.at[parity], act_sem.at[parity]
        )

    def outputs(j):
        if j == 0:
            act_load(0, 0, 0).start()

        def one(p, carry):
            parity = lax.rem(p, 2)
            act_load(j, p, parity).wait()

            @pl.when(p < 3)
            def _():
                act_load(j, p + 1, 1 - parity).start()

            if j + 1 < ranks:

                @pl.when(p == 3)
                def _():
                    act_load(j + 1, 0, 0).start()

            wide = act_buf[parity].reshape(2 * rows, act_buf.shape[3])
            out = plain_dot(wide, down_rows[...])
            blocks[j % 2, pl.ds(2 * p, 2)] = bfloat(out).reshape(2, rows, width)
            return carry

        lax.fori_loop(0, 4, one, 0)
        for kind in (K_CORE_FAR, K_CORE_X, K_CORE_Y, K_CORE_OWN):
            copy_of(kind, j).start()

    def sums_first(j):
        at = blocks.at[j % 2].at
        copy_of(K_CORE_FAR, j).wait_recv()
        add_rows(at[6], rows, core_buf.at[j, 3])
        copy_of(K_FAR_X, j).start()
        copy_of(K_FAR_Y, j).start()
        copy_of(K_CORE_X, j).wait_recv()
        add_rows(at[2, first], half, core_buf.at[j, 1, first])
        copy_of(K_X_FIRST, j).start()
        copy_of(K_CORE_Y, j).wait_recv()
        add_rows(at[3, last], half, core_buf.at[j, 2, last])
        copy_of(K_Y_LAST, j).start()

    def sums_next(j):
        at = blocks.at[j % 2].at
        copy_of(K_FAR_X, j).wait_recv()
        add_rows(at[3, first], half, core_buf.at[j, 2, first], far_buf.at[j, 0])
        copy_of(K_Y_FIRST, j).start()
        copy_of(K_FAR_Y, j).wait_recv()
        add_rows(at[2, last], half, core_buf.at[j, 1, last], far_buf.at[j, 1])
        copy_of(K_X_LAST, j).start()

    def sums_store(j):
        return pltpu.make_async_copy(
            blocks.at[j % 2, 0], moe_sums.at[j], sums_sem.at[j % 2]
        )

    def sums_last(j):
        at = blocks.at[j % 2].at
        for kind in (K_CORE_OWN, K_X_FIRST, K_X_LAST, K_Y_FIRST, K_Y_LAST):
            copy_of(kind, j).wait_recv()
        for n, part in enumerate((first, last)):
            add_rows(at[0, part], half, core_buf.at[j, 0, part], x_buf.at[j, n], y_buf.at[j, n])
        sums_store(j).start()
        for kind in SUM_KINDS:
            copy_of(kind, j).wait_send()
        sums_store(j).wait()

    chunk, columns = right_buf.shape[1:]
    chunks, parts = row_all.shape[0] // chunk, width // columns
    kinds = ((gate_all, gate_out), (up_all, up_out))

    def chunk_loads(w, unit, parity):
        at = pl.ds(pl.multiple_of(lax.rem(unit, chunks) * chunk, chunk), chunk)
        part = pl.ds(pl.multiple_of(lax.div(unit, chunks) * columns, columns), columns)
        return (
            pltpu.make_async_copy(kinds[w][0].at[at], left_buf.at[parity], load_sem.at[parity, 0]),
            pltpu.make_async_copy(
                row_all.at[at, part], right_buf.at[parity], load_sem.at[parity, 1]
            ),
        )

    def acc_store(w, unit):
        part = pl.ds(pl.multiple_of(lax.div(unit, chunks) * columns, columns), columns)
        return (
            pltpu.make_async_copy(
                acc.at[pl.ds(0, routed_width)], kinds[w][1].at[:, part], acc_sem.at[0]
            ),
            pltpu.make_async_copy(
                acc.at[pl.ds(routed_width, shared_pad)], shared_rows.at[w, :, part], acc_sem.at[1]
            ),
        )

    units = chunks * parts

    def products(w, begin, end):
        def one(unit, carry):
            parity = lax.rem(unit, 2)

            @pl.when(unit + 1 < units)
            def _():
                for copy in chunk_loads(w, unit + 1, 1 - parity):
                    copy.start()

            if w + 1 < len(kinds):

                @pl.when(unit + 1 == units)
                def _():
                    for copy in chunk_loads(w + 1, 0, 0):
                        copy.start()

            for copy in chunk_loads(w, unit, parity):
                copy.wait()
            part = first_dot(left_buf[parity], right_buf[parity])
            place = lax.rem(unit, chunks)

            @pl.when(place == 0)
            def _():
                acc[...] = part

            @pl.when(place > 0)
            def _():
                acc[...] += part

            @pl.when(place == chunks - 1)
            def _():
                for copy in acc_store(w, unit):
                    copy.start()
                for copy in acc_store(w, unit):
                    copy.wait()

            return carry

        lax.fori_loop(begin, end, one, 0)

    def attended_piece(r):
        attended_grad[r * rows : (r + 1) * rows, :] = bfloat(
            last_dot(resid_buf[r], output[...])
        )

    def prob_load(h):
        return pltpu.make_async_copy(prob_all.at[h], prob.at[h % 2], prob_sem.at[h % 2])

    def head(h):
        prob_load(h).wait()
        ratio = prob[h % 2]
        back = attended_grad[:, h * VDIM : (h + 1) * VDIM]
        prob_back = last_dot(back, value[h])
        row_dot = jnp.sum(prob_back * ratio, axis=-1, keepdims=True)
        score_back = bfloat(ratio * (prob_back - row_dot))
        value_back = first_dot(bfloat(ratio), back)
        query_back = bfloat(plain_dot(score_back, k_cat[h]) * scaling)
        key_back = bfloat(first_dot(score_back, q_cat[h]) * scaling)
        step = NOPE + VDIM
        expand_grad[:, h * step : h * step + NOPE] = key_back[:, :NOPE]
        expand_grad[:, h * step + NOPE : (h + 1) * step] = bfloat(value_back)
        query_grad[:, h * NOPE : (h + 1) * NOPE] = query_back[:, :NOPE]
        turned = key_back[:, NOPE:].astype(jnp.float32)
        lane = lax.broadcasted_iota(jnp.int32, turned.shape, 1)
        own = (lane < ROPE) if h % 2 == 0 else (lane >= ROPE)
        key_rot[...] += jnp.where(own, turned, 0.0)
        rope_part = query_back[:, NOPE:].astype(jnp.float32)
        if h % 2 == 0:
            pair[...] = rope_part
        else:
            whole = pair[...] + rope_part
            start = heads * NOPE + h // 2 * lanes
            query_grad[:, start : start + lanes] = bfloat(
                turn(whole, cos_table[...], -sin_table[...])
            )
        if h + 2 < heads:
            prob_load(h + 2).start()

    prob_load(0).start()
    prob_load(1).start()
    for copy in chunk_loads(0, 0, 0):
        copy.start()
    for copy in local[1:]:
        copy.wait()
    outputs(0)
    local[0].wait()
    attended_piece(0)
    sums_first(0)
    resid_step(0).wait_recv()
    resid_step(1).start()
    attended_piece(1)
    outputs(1)
    sums_next(0)
    sums_first(1)
    products(0, 0, 3)
    resid_step(1).wait_recv()
    resid_step(2).start()
    attended_piece(2)
    sums_last(0)
    outputs(2)
    sums_next(1)
    sums_first(2)
    products(0, 3, 5)
    resid_step(2).wait_recv()
    save = pltpu.make_async_copy(resid_buf, resid_all, local_sem.at[3])
    save.start()
    attended_piece(3)
    for h in range(heads):
        head(h)

    folded = key_rot[...] + pltpu.roll(key_rot[...], ROPE, 1)
    key_rot[...] = folded

    def partial(r):
        at = slice(r * rows, (r + 1) * rows)
        latent = last_dot(expand_grad[at, :], expand[...])
        normed = last_dot(query_grad[at, :], query[...])
        return normed, latent, key_rot[at, :]

    splits = ((0, width), (width, width + LATENT), (width + LATENT, width + LATENT + lanes))

    def ring_step(step):
        return remote(
            ring_out.at[step], ring_buf.at[step], ring_send.at[step], ring_recv.at[step], right
        )

    def between_0():
        sums_last(1)
        outputs(3)
        sums_next(2)
        sums_first(3)
        products(0, 5, 8)

    def between_1():
        sums_last(2)
        sums_next(3)
        products(0, 8, 16)

    def between_2():
        sums_last(3)
        products(1, 0, 8)

    for step, between in enumerate((between_0, between_1, between_2)):
        values = partial(step + 1)
        if step:
            ring_step(step - 1).wait_recv()
        for (start, stop), part in zip(splits, values):
            if step:
                part = part + ring_buf[step - 1, :, start:stop].astype(jnp.float32)
            ring_out[step, :, start:stop] = bfloat(part)
        ring_step(step).start()
        between()
    parts = partial(0)
    ring_step(ranks - 2).wait_recv()
    normed_back[...] = parts[0] + ring_buf[ranks - 2, :, :width].astype(jnp.float32)
    latent_back[:, :LATENT] = parts[1] + ring_buf[
        ranks - 2, :, width : width + LATENT
    ].astype(jnp.float32)
    latent_back[:, LATENT:] = parts[2] + ring_buf[ranks - 2, :, width + LATENT :].astype(
        jnp.float32
    )
    products(1, 8, 16)
    save.wait()
    for step in range(ranks - 1):
        resid_step(step).wait_send()
        ring_step(step).wait_send()


def back_pass(
    resid,
    acts,
    expert_down,
    shared_all,
    output,
    query,
    expand,
    q_cat,
    k_cat,
    value,
    prob_all,
    cos_table,
    sin_table,
    gate_all,
    up_all,
    row_all,
):
    ranks, groups = lax.axis_size(TENSOR), lax.axis_size(DP)
    rows, width = resid.shape
    group_rows = rows * ranks
    heads = q_cat.shape[0]
    lanes = cos_table.shape[1]
    hidden_width = acts.shape[-1]
    low, full = jnp.bfloat16, jnp.float32
    anywhere = pl.BlockSpec(memory_space=pl.ANY)
    in_vmem = pl.BlockSpec(memory_space=pltpu.VMEM)
    dma = pltpu.SemaphoreType.DMA

    def array(*shape, dtype=low):
        return jax.ShapeDtypeStruct(shape, dtype)

    return pl.pallas_call(
        back_kernel,
        out_shape=(
            array(ranks, rows, width),
            array(ranks, rows, width),
            array(expert_down.shape[0], width, dtype=full),
            array(expert_down.shape[0], width, dtype=full),
            array(2, shared_all.shape[1], width, dtype=full),
            array(rows, width, dtype=full),
            array(rows, LATENT + lanes, dtype=full),
            array(group_rows, query.shape[1]),
            array(group_rows, expand.shape[1]),
        ),
        in_specs=[anywhere] * 4 + [in_vmem] * 6 + [anywhere] + [in_vmem] * 2 + [anywhere] * 3,
        out_specs=(anywhere,) * 5 + (in_vmem,) * 4,
        scratch_shapes=[
            pltpu.VMEM((hidden_width, width), low),
            pltpu.VMEM((2, 2, rows, hidden_width), low),
            pltpu.VMEM((ranks, rows, width), low),
            pltpu.VMEM((group_rows, heads * VDIM), low),
            pltpu.VMEM((2, group_rows, group_rows), full),
            pltpu.VMEM((group_rows, lanes), full),
            pltpu.VMEM((group_rows, lanes), full),
            pltpu.VMEM((2, groups, rows, width), low),
            pltpu.VMEM((ranks, 4, rows, width), low),
            pltpu.VMEM((ranks, 2, rows // 2, width), low),
            pltpu.VMEM((ranks, 2, rows // 2, width), low),
            pltpu.VMEM((ranks, 2, rows // 2, width), low),
            pltpu.VMEM((ranks - 1, rows, width + LATENT + lanes), low),
            pltpu.VMEM((ranks - 1, rows, width + LATENT + lanes), low),
            pltpu.VMEM((2, 512, hidden_width), low),
            pltpu.VMEM((2, 512, width // 2), low),
            pltpu.VMEM((hidden_width, width // 2), full),
            dma((4,)),
            dma((2,)),
            dma((2,)),
            dma((2,)),
            dma((2, 2)),
            dma((2,)),
            dma((ranks - 1,)),
            dma((ranks - 1,)),
            dma((10, ranks)),
            dma((10, ranks)),
            dma((ranks - 1,)),
            dma((ranks - 1,)),
        ],
        compiler_params=pltpu.CompilerParams(
            collective_id=3, has_side_effects=True, vmem_limit_bytes=63 * 1024 * 1024
        ),
        name="back_pass",
    )(
        resid,
        acts,
        expert_down,
        shared_all,
        output,
        query,
        expand,
        q_cat,
        k_cat,
        value,
        prob_all,
        cos_table,
        sin_table,
        gate_all,
        up_all,
        row_all,
    )


def weight_kernel(
    normed_in,
    latent_group_in,
    attended_in,
    resid_in,
    query_grad_in,
    expand_grad_in,
    normed_back,
    latent_back,
    own_latent,
    hidden_in,
    resid_grad_in,
    residual_in,
    cos_table,
    sin_table,
    attn_gain,
    latent_gain,
    mlp_grad,
    latent_columns_in,
    moe_sums,
    shared_rows,
    act_all,
    cotan_all,
    layer_out,
    hidden_grad,
    query_out,
    expand_out,
    output_out,
    gains_out,
    latent_all,
    shared_gate_out,
    shared_up_out,
    shared_down_out,
    down_out,
    query_full,
    expand_full,
    output_full,
    core_q,
    core_e,
    core_o,
    far_q,
    far_e,
    far_o,
    x_q,
    x_e,
    x_o,
    y_q,
    y_e,
    y_o,
    gains,
    latent_own,
    latent_rows,
    latent_full,
    latent_buf,
    latent_piece,
    gains_buf,
    gains_sum,
    gains_rank,
    act_buf,
    cotan_buf,
    acc,
    shared_full,
    shared_low,
    shared_back,
    moe_first,
    moe_out,
    moe_in,
    normed,
    attended,
    resid,
    query_grad,
    expand_grad,
    latent_group,
    hidden,
    resid_grad,
    residual,
    latent_columns,
    stage_sem,
    load_sem,
    local_sem,
    out_sem,
    s_send,
    s_recv,
    lz_send,
    lz_recv,
    ld_send,
    ld_recv,
    lp_send,
    lp_recv,
    lc_send,
    lc_recv,
    gd_send,
    gd_recv,
    gz_send,
    gz_recv,
    h_send,
    h_recv,
    m_send,
    m_recv,
):
    me, rank = lax.axis_index(DP), lax.axis_index(TENSOR)
    ranks, count = lax.axis_size(TENSOR), lax.axis_size(DP)
    by_core, by_x, by_y = [(flip(me, bit), rank) for bit in (1, 2, 4)]

    def owner(k):
        other = me
        for bit in (1, 2, 4):
            other = flip(other, bit) if k & bit else other
        return other

    partners = [(owner(k), rank) for k in range(1, count)]
    beside = [(me, lax.rem(rank + r, ranks)) for r in range(1, ranks)]
    width = normed.shape[1]
    routed_width = down_out.shape[0]
    shared_pad = shared_low.shape[1]
    rows = hidden.shape[0]
    staged = {}
    for n, (key, src, dst) in enumerate(
        (
            (0, normed_in, normed),
            (1, query_grad_in, query_grad),
            (2, latent_columns_in, latent_columns),
            (2, hidden_in, hidden),
            (2, resid_grad_in, resid_grad),
            (3, attended_in, attended),
            (3, resid_in, resid),
            (4, latent_group_in, latent_group),
            (4, expand_grad_in, expand_grad),
            (5, residual_in, residual),
        )
    ):
        copy = pltpu.make_async_copy(src, dst, stage_sem.at[n])
        copy.start()
        staged.setdefault(key, []).append(copy)

    def ready(key):
        for copy in staged[key]:
            copy.wait()

    greet(partners + beside)

    def moe_step(step):
        src = moe_sums.at[1] if step == 0 else moe_out.at[step]
        return remote(src, moe_in.at[step], m_send.at[step], m_recv.at[step], beside[0])

    moe_loads = [
        pltpu.make_async_copy(moe_sums.at[0], moe_first, local_sem.at[4]),
        pltpu.make_async_copy(moe_sums.at[2], moe_out.at[1], local_sem.at[5]),
        pltpu.make_async_copy(moe_sums.at[3], moe_out.at[2], local_sem.at[6]),
    ]
    shared_load = pltpu.make_async_copy(shared_rows, shared_full, local_sem.at[7])
    for copy in moe_loads + [shared_load]:
        copy.start()

    def moe_next(step):
        moe_loads[step].wait()
        moe_step(step - 1).wait_recv()
        add_rows(moe_out.at[step], rows, moe_in.at[step - 1])
        moe_step(step).start()

    def moe_last():
        ready(5)
        moe_loads[0].wait()
        moe_step(ranks - 2).wait_recv()
        total = moe_first[...].astype(jnp.float32) + moe_in[ranks - 2].astype(jnp.float32)
        layer_out[...] = bfloat(residual[...] + total)

    values = own_latent[...]
    scale = lax.rsqrt(jnp.mean(values * values, axis=-1, keepdims=True) + epsilon)
    grad = latent_back[:, :LATENT]
    scaled_grad = grad * latent_gain[...]
    inner = jnp.mean(scaled_grad * values, axis=-1, keepdims=True)
    latent_in = scale * scaled_grad - values * (scale * scale * scale) * inner
    latent_own[:, :LATENT] = bfloat(latent_in)
    latent_own[:, LATENT:] = bfloat(
        turn(latent_back[:, LATENT:], cos_table[0:rows, :], -sin_table[0:rows, :])
    )
    gains[...] = jnp.zeros_like(gains)
    gains[2:3, :LATENT] = jnp.sum(grad * values * scale, axis=0, keepdims=True)
    gains[1:2, :] = mlp_grad[...]

    def first_norm():
        ready(2)
        lanes = latent_columns.shape[0]
        total = normed_back[...] + plain_dot(latent_own[:, :lanes], latent_columns[...])
        values = hidden[...].astype(jnp.float32)
        scale = lax.rsqrt(jnp.mean(values * values, axis=-1, keepdims=True) + epsilon)
        scaled_grad = total * attn_gain[...]
        inner = jnp.mean(scaled_grad * values, axis=-1, keepdims=True)
        through = scale * scaled_grad - values * (scale * scale * scale) * inner
        hidden_grad[...] = resid_grad[...] + through
        gains[0:1, :] = jnp.sum(total * values * scale, axis=0, keepdims=True)

    own_rows = pltpu.make_async_copy(latent_own, latent_rows.at[0], local_sem.at[0])
    own_rows.start()
    latent_sends = [
        remote(latent_own, latent_rows.at[r], lz_send.at[r - 1], lz_recv.at[r - 1], peer)
        for r, peer in enumerate(beside, 1)
    ]
    gains_sends = [
        remote(gains, gains_buf.at[me], gd_send.at[n], gd_recv.at[n], peer)
        for n, peer in enumerate(partners)
    ]
    for copy in latent_sends:
        copy.start()

    sets = (
        (query_full, core_q, far_q, x_q, y_q, query_out),
        (expand_full, core_e, far_e, x_e, y_e, expand_out),
        (output_full, core_o, far_o, x_o, y_o, output_out),
    )

    def copy_of(i, kind):
        whole, core, far, x_buf, y_buf, _ = sets[i]
        half = whole.shape[1] // 2
        first, last = pl.ds(0, half), pl.ds(half, half)
        at = whole.at
        n, src, dst, peer = {
            K_CORE_OWN: lambda: (0, at[owner(1)], core.at[0], by_core),
            K_CORE_X: lambda: (1, at[owner(3)], core.at[1], by_core),
            K_CORE_Y: lambda: (2, at[owner(5)], core.at[2], by_core),
            K_CORE_FAR: lambda: (3, at[owner(7)], core.at[3], by_core),
            K_FAR_X: lambda: (4, at[owner(6), first], far.at[0], by_x),
            K_FAR_Y: lambda: (5, at[owner(6), last], far.at[1], by_y),
            K_X_FIRST: lambda: (6, at[owner(2), first], x_buf.at[0], by_x),
            K_X_LAST: lambda: (7, at[owner(2), last], x_buf.at[1], by_x),
            K_Y_FIRST: lambda: (8, at[owner(4), first], y_buf.at[0], by_y),
            K_Y_LAST: lambda: (9, at[owner(4), last], y_buf.at[1], by_y),
        }[kind]()
        return remote(src, dst, s_send.at[i, n], s_recv.at[i, n], peer)

    def sums_start(i):
        for kind in (K_CORE_FAR, K_CORE_X, K_CORE_Y, K_CORE_OWN):
            copy_of(i, kind).start()

    def sums_first(i):
        whole, core, _, _, _, _ = sets[i]
        half = whole.shape[1] // 2
        first, last = pl.ds(0, half), pl.ds(half, half)
        copy_of(i, K_CORE_FAR).wait_recv()
        add_rows(whole.at[owner(6)], 2 * half, core.at[3])
        copy_of(i, K_FAR_X).start()
        copy_of(i, K_FAR_Y).start()
        copy_of(i, K_CORE_X).wait_recv()
        add_rows(whole.at[owner(2), first], half, core.at[1, first])
        copy_of(i, K_X_FIRST).start()
        copy_of(i, K_CORE_Y).wait_recv()
        add_rows(whole.at[owner(4), last], half, core.at[2, last])
        copy_of(i, K_Y_LAST).start()

    def sums_next(i):
        whole, core, far, _, _, _ = sets[i]
        half = whole.shape[1] // 2
        first, last = pl.ds(0, half), pl.ds(half, half)
        copy_of(i, K_FAR_X).wait_recv()
        add_rows(whole.at[owner(4), first], half, core.at[2, first], far.at[0])
        copy_of(i, K_Y_FIRST).start()
        copy_of(i, K_FAR_Y).wait_recv()
        add_rows(whole.at[owner(2), last], half, core.at[1, last], far.at[1])
        copy_of(i, K_X_LAST).start()

    def sums_last(i):
        whole, core, _, x_buf, y_buf, out = sets[i]
        half = whole.shape[1] // 2
        for kind in (K_CORE_OWN, K_X_FIRST, K_X_LAST, K_Y_FIRST, K_Y_LAST):
            copy_of(i, kind).wait_recv()
        for n in range(2):
            part = pl.ds(n * half, half)
            add_rows(
                whole.at[me, part],
                half,
                core.at[0, part],
                x_buf.at[n],
                y_buf.at[n],
                store=out.at[part],
            )

    q_rows, o_cols = query_full.shape[1], output_full.shape[2]
    ready(0)
    ready(1)
    for o in range(count):
        at = slice(o * q_rows, (o + 1) * q_rows)
        query_full[o] = bfloat(first_dot(normed[:, at], query_grad[...]))
    sums_start(0)

    part_width = latent_full.shape[2]
    latent_count = latent_full.shape[1]
    own_rows.wait()
    for copy in latent_sends:
        copy.wait_recv()
    columns = pl.ds(pl.multiple_of(rank * part_width, part_width), part_width)
    rows_low = latent_rows[...].reshape(-1, latent_rows.shape[2])
    latent_full[...] = bfloat(first_dot(rows_low, normed[:, columns])).reshape(latent_full.shape)
    dealt = [
        remote(
            latent_full.at[peer[0]], latent_buf.at[me], ld_send.at[n], ld_recv.at[n], peer
        )
        for n, peer in enumerate(partners)
    ]
    for copy in dealt:
        copy.start()
    moe_step(0).start()
    latent_buf[me] = latent_full[me]
    first_norm()
    for copy in gains_sends:
        copy.start()
    gains_buf[me] = gains[...]
    ready(3)
    for o in range(count):
        at = slice(o * o_cols, (o + 1) * o_cols)
        output_full[o] = bfloat(first_dot(attended[...], resid[:, at]))
    sums_start(2)
    ready(4)
    expanded = bfloat(first_dot(latent_group[...], expand_grad[...]))
    expand_full[...] = expanded.reshape(expand_full.shape)
    sums_start(1)

    def latent_at(o, columns=None):
        at = pl.ds(pl.multiple_of(o * latent_count, latent_count), latent_count)
        return latent_all.at[at] if columns is None else latent_all.at[at, columns]

    pieces = [
        remote(
            latent_piece, latent_at(me, columns), lp_send.at[r - 1], lp_recv.at[r - 1], peer
        )
        for r, peer in enumerate(beside, 1)
    ]
    own_piece = pltpu.make_async_copy(latent_piece, latent_at(me, columns), local_sem.at[1])

    def latent_sum():
        for copy in dealt:
            copy.wait_recv()
        total = latent_buf[0].astype(jnp.float32)
        for o in range(1, count):
            total = total + latent_buf[o].astype(jnp.float32)
        latent_piece[...] = bfloat(total)
        for copy in pieces + [own_piece]:
            copy.start()

    def latent_copy(kind):
        first, last = pl.ds(0, width // 2), pl.ds(width // 2, width // 2)
        n, block, peer = {
            K_X: lambda: (0, latent_at(me), by_x),
            K_Y: lambda: (1, latent_at(me), by_y),
            K_CORE: lambda: (2, latent_at(me), by_core),
            K_FAR_Y: lambda: (3, latent_at(owner(2), last), by_y),
            K_FAR_X: lambda: (4, latent_at(owner(4), first), by_x),
            K_CORE_X: lambda: (5, latent_at(owner(2)), by_core),
            K_CORE_Y: lambda: (6, latent_at(owner(4)), by_core),
            K_CORE_FAR: lambda: (7, latent_at(owner(6)), by_core),
        }[kind]()
        return remote(block, block, lc_send.at[n], lc_recv.at[n], peer)

    def latent_cube():
        own_piece.wait()
        for copy in pieces:
            copy.wait_recv()
        for kind in (K_X, K_Y, K_CORE):
            latent_copy(kind).start()

    def latent_forward():
        latent_copy(K_X).wait_recv()
        latent_copy(K_FAR_Y).start()
        latent_copy(K_CORE_X).start()
        latent_copy(K_Y).wait_recv()
        latent_copy(K_FAR_X).start()
        latent_copy(K_CORE_Y).start()

    def latent_far():
        latent_copy(K_FAR_X).wait_recv()
        latent_copy(K_FAR_Y).wait_recv()
        latent_copy(K_CORE_FAR).start()

    gains_beside = [
        remote(gains_sum, gains_rank.at[rank], gz_send.at[r - 1], gz_recv.at[r - 1], peer)
        for r, peer in enumerate(beside, 1)
    ]

    def gains_first():
        for copy in gains_sends:
            copy.wait_recv()
        total = gains_buf[0]
        for o in range(1, count):
            total = total + gains_buf[o]
        gains_sum[...] = total
        gains_rank[rank] = total
        for copy in gains_beside:
            copy.start()

    def gains_last():
        for copy in gains_beside:
            copy.wait_recv()
        total = gains_rank[0]
        for r in range(1, ranks):
            total = total + gains_rank[r]
        gains_out[...] = total

    chunk, columns = cotan_buf.shape[1:]
    chunks = cotan_all.shape[0] // chunk
    units = chunks * (width // columns)

    def loads(unit, parity):
        at = pl.ds(pl.multiple_of(lax.rem(unit, chunks) * chunk, chunk), chunk)
        part = pl.ds(pl.multiple_of(lax.div(unit, chunks) * columns, columns), columns)
        return (
            pltpu.make_async_copy(act_all.at[at], act_buf.at[parity], load_sem.at[parity, 0]),
            pltpu.make_async_copy(
                cotan_all.at[at, part], cotan_buf.at[parity], load_sem.at[parity, 1]
            ),
        )

    def acc_store(unit):
        part = pl.ds(pl.multiple_of(lax.div(unit, chunks) * columns, columns), columns)
        return pltpu.make_async_copy(
            acc.at[pl.ds(0, routed_width)], down_out.at[:, part], out_sem
        )

    def products(begin, end):
        def one(unit, carry):
            parity = lax.rem(unit, 2)

            @pl.when(unit + 1 < units)
            def _():
                for copy in loads(unit + 1, 1 - parity):
                    copy.start()

            for copy in loads(unit, parity):
                copy.wait()
            part = first_dot(act_buf[parity], cotan_buf[parity])
            place = lax.rem(unit, chunks)

            @pl.when(place == 0)
            def _():
                acc[...] = part

            @pl.when(place > 0)
            def _():
                acc[...] += part

            @pl.when(place == chunks - 1)
            def _():
                acc_store(unit).start()
                start = pl.multiple_of(lax.div(unit, chunks) * columns, columns)
                shared_low[2, :, pl.ds(start, columns)] = bfloat(
                    acc[routed_width : routed_width + shared_pad, :]
                )
                acc_store(unit).wait()

            return carry

        lax.fori_loop(begin, end, one, 0)

    def shared_copies(at, n):
        size = shared_back.shape[3]
        return [
            remote(
                shared_low.at[at, :, pl.ds(pl.multiple_of(peer[0] * size, size), size)],
                shared_back.at[me, at],
                h_send.at[n, m],
                h_recv.at[n, m],
                peer,
            )
            for m, peer in enumerate(partners)
        ]

    def own_shared(at, n):
        size = shared_back.shape[3]
        return pltpu.make_async_copy(
            shared_low.at[at, :, pl.ds(pl.multiple_of(me * size, size), size)],
            shared_back.at[me, at],
            local_sem.at[2 + n],
        )

    def shared_receive(at, n, outs):
        own_shared(at, n).wait()
        for copy in shared_copies(at, n):
            copy.wait_recv()
        for m, out in outs:
            size = out.shape[0] // count
            for o in range(count):
                out[o * size : (o + 1) * size, :] = shared_back[o, m, :size, :].astype(jnp.float32)

    for copy in loads(0, 0):
        copy.start()
    pair, single = pl.ds(0, 2), pl.ds(2, 1)
    sums_first(0)
    sums_first(2)
    sums_first(1)
    latent_sum()
    products(0, 3)
    moe_next(1)
    latent_cube()
    sums_next(0)
    sums_next(2)
    sums_next(1)
    gains_first()
    products(3, 5)
    latent_forward()
    moe_next(2)
    latent_far()
    shared_load.wait()
    shared_low[0:2] = bfloat(shared_full[...])
    for copy in shared_copies(pair, 0) + [own_shared(pair, 0)]:
        copy.start()
    products(5, 8)
    for i in (0, 2, 1):
        sums_last(i)
    gains_last()
    products(8, 16)
    for copy in shared_copies(single, 1) + [own_shared(single, 1)]:
        copy.start()
    moe_last()
    for kind in (K_CORE, K_CORE_X, K_CORE_Y, K_CORE_FAR):
        latent_copy(kind).wait_recv()
    shared_receive(pair, 0, ((0, shared_gate_out), (1, shared_up_out)))
    shared_receive(single, 1, ((2, shared_down_out),))

    for kind in (K_X, K_Y, K_CORE, K_FAR_Y, K_FAR_X, K_CORE_X, K_CORE_Y, K_CORE_FAR):
        latent_copy(kind).wait_send()
    for copy in latent_sends + gains_sends + dealt + pieces + gains_beside:
        copy.wait_send()
    for i in range(len(sets)):
        for kind in SUM_KINDS:
            copy_of(i, kind).wait_send()
    for step in range(ranks - 1):
        moe_step(step).wait_send()
    for at, n in ((pair, 0), (single, 1)):
        for copy in shared_copies(at, n):
            copy.wait_send()


def weight_pass(
    normed,
    latent_group,
    attended,
    resid,
    query_grad,
    expand_grad,
    normed_back,
    latent_back,
    own_latent,
    hidden,
    resid_grad,
    residual,
    cos_table,
    sin_table,
    attn_gain,
    latent_gain,
    mlp_grad,
    latent_columns,
    moe_sums,
    shared_rows,
    act_all,
    cotan_all,
    shared_width,
    routed_width,
):
    ranks, count = lax.axis_size(TENSOR), lax.axis_size(DP)
    rows, width = hidden.shape
    hidden_width = act_all.shape[1]
    shared_pad = shared_rows.shape[1]
    low, full = jnp.bfloat16, jnp.float32
    anywhere = pl.BlockSpec(memory_space=pl.ANY)
    in_vmem = pl.BlockSpec(memory_space=pltpu.VMEM)
    dma = pltpu.SemaphoreType.DMA
    chunk = cotan_all.shape[0] // 8
    latent_width = latent_back.shape[1]
    q_shape = (width // count, query_grad.shape[1])
    e_shape = (latent_group.shape[1] // count, expand_grad.shape[1])
    o_shape = (attended.shape[1], width // count)
    l_shape = (latent_width // count, width // ranks)
    g_shape = (8, width)
    shapes = (q_shape, e_shape, o_shape)

    def array(*shape):
        return jax.ShapeDtypeStruct(shape, full)

    def halves(n):
        return [pltpu.VMEM((n, shape[0] // 2, shape[1]), low) for shape in shapes]

    return pl.pallas_call(
        weight_kernel,
        out_shape=(
            jax.ShapeDtypeStruct((rows, width), low),
            array(rows, width),
            array(*q_shape),
            array(*e_shape),
            array(*o_shape),
            array(*g_shape),
            jax.ShapeDtypeStruct((latent_width, width), low),
            array(count * shared_width, width // count),
            array(count * shared_width, width // count),
            array(count * shared_width, width // count),
            array(routed_width, width),
        ),
        in_specs=[anywhere] * 6
        + [in_vmem] * 3
        + [anywhere] * 3
        + [in_vmem] * 5
        + [anywhere] * 5,
        out_specs=(in_vmem,) * 6 + (anywhere,) + (in_vmem,) * 3 + (anywhere,),
        scratch_shapes=[pltpu.VMEM((count,) + shape, low) for shape in shapes]
        + [pltpu.VMEM((4,) + shape, low) for shape in shapes]
        + halves(2)
        + halves(2)
        + halves(2)
        + [
            pltpu.VMEM(g_shape, full),
            pltpu.VMEM((rows, latent_width), low),
            pltpu.VMEM((ranks, rows, latent_width), low),
            pltpu.VMEM((count,) + l_shape, low),
            pltpu.VMEM((count,) + l_shape, low),
            pltpu.VMEM(l_shape, low),
            pltpu.VMEM((count,) + g_shape, full),
            pltpu.VMEM(g_shape, full),
            pltpu.VMEM((ranks,) + g_shape, full),
            pltpu.VMEM((2, chunk, hidden_width), low),
            pltpu.VMEM((2, chunk, width // 2), low),
            pltpu.VMEM((hidden_width, width // 2), full),
            pltpu.VMEM((2, shared_pad, width), full),
            pltpu.VMEM((3, shared_pad, width), low),
            pltpu.VMEM((count, 3, shared_pad, width // count), low),
            pltpu.VMEM((rows, width), low),
            pltpu.VMEM((ranks - 1, rows, width), low),
            pltpu.VMEM((ranks - 1, rows, width), low),
        ]
        + [
            pltpu.VMEM(values.shape, values.dtype)
            for values in (
                normed,
                attended,
                resid,
                query_grad,
                expand_grad,
                latent_group,
                hidden,
                resid_grad,
                residual,
                latent_columns,
            )
        ]
        + [
            dma((10,)),
            dma((2, 2)),
            dma((8,)),
            dma,
            dma((3, 10)),
            dma((3, 10)),
            dma((ranks - 1,)),
            dma((ranks - 1,)),
            dma((count - 1,)),
            dma((count - 1,)),
            dma((ranks - 1,)),
            dma((ranks - 1,)),
            dma((8,)),
            dma((8,)),
            dma((count - 1,)),
            dma((count - 1,)),
            dma((ranks - 1,)),
            dma((ranks - 1,)),
            dma((2, count - 1)),
            dma((2, count - 1)),
            dma((ranks - 1,)),
            dma((ranks - 1,)),
        ],
        compiler_params=pltpu.CompilerParams(
            collective_id=4, has_side_effects=True, vmem_limit_bytes=63 * 1024 * 1024
        ),
        name="weight_pass",
    )(
        normed,
        latent_group,
        attended,
        resid,
        query_grad,
        expand_grad,
        normed_back,
        latent_back,
        own_latent,
        hidden,
        resid_grad,
        residual,
        cos_table,
        sin_table,
        attn_gain,
        latent_gain,
        mlp_grad,
        latent_columns,
        moe_sums,
        shared_rows,
        act_all,
        cotan_all,
    )


def part_heads(values, heads):
    split = values.reshape(-1, heads, NOPE + ROPE)
    parts = (split[:, :, :NOPE], split[:, :, NOPE:])
    return jnp.concatenate([part.reshape(values.shape[0], -1) for part in parts], axis=1)


def join_heads(values, heads):
    plain = values[:, : heads * NOPE].reshape(-1, heads, NOPE)
    turned = values[:, heads * NOPE :].reshape(-1, heads, ROPE)
    return jnp.concatenate([plain, turned], axis=2).reshape(values.shape)


def cube_shards(
    hidden,
    cotangent,
    routes,
    route_gates,
    doc_lengths,
    attn_gain,
    query_weight,
    latent_weight,
    latent_gain,
    expand_weight,
    output_weight,
    mlp_gain,
    shared_gate,
    shared_up,
    shared_down,
    expert_gate,
    expert_up,
    expert_down,
):
    ranks = lax.axis_size(TENSOR)
    groups = lax.axis_size(DP)
    rows = hidden.shape[0]
    group_rows = rows * ranks
    width = hidden.shape[1]
    local_experts, _, expert_width = expert_gate.shape
    experts = local_experts * groups

    shared_width = shared_gate.shape[1] // groups
    shared_pad = -(-shared_width // 16) * 16
    shared_stack = jnp.stack(
        [
            jnp.pad(
                weight.reshape(groups, shared_width, weight.shape[1]),
                ((0, 0), (0, shared_pad - shared_width), (0, 0)),
            )
            for weight in (shared_gate.T, shared_up.T, shared_down)
        ],
        axis=1,
    )
    routed_width = local_experts * expert_width
    hidden_width = -(-(routed_width + shared_pad) // 128) * 128
    local_heads = query_weight.shape[1] // (NOPE + ROPE)
    latent_columns = latent_weight.T

    (
        normed_group,
        latent_group,
        own_latent,
        query_full,
        expand_full,
        output_full,
        q_cat,
        k_cat,
        value_all,
        probability,
        attended_low,
        cos_group,
        sin_group,
        residual,
        normed_two,
        shared_all,
        slot_gates,
        cotan_all,
        back_all,
    ) = front_pass(
        doc_lengths,
        hidden,
        cotangent,
        part_heads(query_weight, local_heads),
        expand_weight,
        output_weight,
        shared_stack,
        expert_down.reshape(-1, width),
        routes.T,
        route_gates.T,
        jnp.concatenate([latent_columns, latent_columns[LATENT:]], axis=0),
        attn_gain[None],
        latent_gain[None],
        mlp_gain[None],
        hidden_width,
        experts,
    )
    (
        row_all,
        act_all,
        gate_all,
        up_all,
        resid_grad,
        resid_low,
        mlpgain_part,
    ) = moe_pass(
        normed_two,
        back_all,
        slot_gates,
        expert_gate.transpose(0, 2, 1).reshape(-1, width),
        expert_up.transpose(0, 2, 1).reshape(-1, width),
        shared_all,
        residual,
        cotangent,
        mlp_gain[None],
        expert_width,
    )
    (
        resid_all,
        moe_sums,
        gate_wgrad,
        up_wgrad,
        shared_rows,
        normed_back,
        latent_back,
        qraw_grad,
        expand_rows,
    ) = back_pass(
        resid_low,
        act_all,
        expert_down.reshape(-1, width),
        shared_all,
        output_full,
        query_full,
        expand_full,
        q_cat,
        k_cat,
        value_all,
        probability,
        cos_group,
        sin_group,
        gate_all.reshape(-1, hidden_width),
        up_all.reshape(-1, hidden_width),
        row_all.reshape(-1, width),
    )
    (
        layer_out,
        hidden_grad,
        query_total,
        expand_total,
        output_total,
        small,
        latent_total,
        shared_gate_total,
        shared_up_total,
        shared_down_total,
        down_wgrad,
    ) = weight_pass(
        normed_group,
        latent_group,
        attended_low,
        resid_all.reshape(group_rows, width),
        qraw_grad,
        expand_rows,
        normed_back,
        latent_back,
        own_latent,
        hidden,
        resid_grad,
        residual,
        cos_group,
        sin_group,
        attn_gain[None],
        latent_gain[None],
        mlpgain_part,
        latent_columns,
        moe_sums,
        shared_rows,
        act_all.reshape(-1, hidden_width),
        cotan_all.reshape(-1, width),
        shared_width,
        routed_width,
    )

    def expert_part(values):
        return values.reshape(local_experts, expert_width, width)

    return (
        layer_out,
        hidden_grad,
        small[0],
        join_heads(query_total, local_heads),
        latent_total[: LATENT + ROPE].T.astype(jnp.float32),
        small[2, :LATENT],
        expand_total,
        output_total,
        small[1],
        shared_gate_total.T,
        shared_up_total.T,
        shared_down_total,
        expert_part(gate_wgrad).transpose(0, 2, 1),
        expert_part(up_wgrad).transpose(0, 2, 1),
        expert_part(down_wgrad),
    )


def solution(mesh):
    in_specs = (
        P((DP, TENSOR), None),
        P((DP, TENSOR), None),
        P(DP, None),
        P(DP, None),
        P(DP, None),
        P(),
        P(DP, TENSOR),
        P(),
        P(),
        P(DP, TENSOR),
        P(TENSOR, DP),
        P(),
        P(DP, TENSOR),
        P(DP, TENSOR),
        P(TENSOR, DP),
        P(DP, None, TENSOR),
        P(DP, None, TENSOR),
        P(DP, TENSOR, None),
    )
    out_specs = (
        P((DP, TENSOR), None),
        P((DP, TENSOR), None),
        P(),
        P(DP, TENSOR),
        P(),
        P(),
        P(DP, TENSOR),
        P(TENSOR, DP),
        P(),
        P(DP, TENSOR),
        P(DP, TENSOR),
        P(TENSOR, DP),
        P(DP, None, TENSOR),
        P(DP, None, TENSOR),
        P(DP, TENSOR, None),
    )
    cube = dict(mesh.shape) == {DP: 8, TENSOR: 4}
    shards = cube_shards if cube else general_shards
    return jax.shard_map(shards, mesh=mesh, in_specs=in_specs, out_specs=out_specs, check_vma=False)
```

profile of v0, /device:TPU:9, one launch (start us, length us, event | category | flops | bytes accessed | tf_op | source)
XLA Modules:
  0.0 574.9 jit_solution(3629299667169837982)
XLA Ops:
  1.3 1.0 slice.38
  2.2 1.2 copy.33
  4.5 1.2 pad_bitcast_fusion
  5.7 1.1 pad_maximum_fusion.1.shared
  6.9 1.7 pad_maximum_fusion.latent_rows
  8.5 137.4 %front_pass.1 = (bf16[512,2048]{1,0:T(8,128)(2,1)}, bf16[512,512]{1,0:T(8,128)(2,1)}, f32[128,512]{1,0:T(8,128)}, bf16[2048,768]{1,0:T(8,128)(2,1)}, bf16[512,10...) custom-call(s32[1,3]{1,0:T(1,128)} %lengths.1, ...), custom_call_target="tpu_custom_call" | custom-call | tf_op jit(solution)/shard_map/front_pass/pallas_call | solution.py:1672
  145.9 166.8 %moe_pass.1 = (bf16[8,4,128,2048]{3,2,1,0:T(8,128)(2,1)}, bf16[8,4,128,896]{3,2,1,0:T(8,128)(2,1)}, bf16[8,4,128,896]{3,2,1,0:T(8,128)(2,1)}, bf16[8,4,128,896]{...) custom-call(bf16[128,2048]{1,0:T(8,128)(2,1)} %get-tuple-element.64.rows, ...), custom_call_target="tpu_custom_call" | custom-call | tf_op jit(solution)/shard_map/moe_pass/pallas_call | solution.py:1050
  312.7 126.8 %back_pass.1 = (bf16[4,128,2048]{2,1,0:T(8,128)(2,1)}, bf16[4,128,2048]{2,1,0:T(8,128)(2,1)}, f32[704,2048]{1,0:T(8,128)}, f32[704,2048]{1,0:T(8,128)}, f32[2,96...) custom-call(bf16[128,2048]{1,0:T(8,128)(2,1)} %get-tuple-element.69., ...), custom_call_target="tpu_custom_call" | custom-call | tf_op jit(solution)/shard_map/back_pass/pallas_call | solution.py:2156
  439.6 105.6 %weight_pass.1 = (bf16[128,2048]{1,0:T(8,128)(2,1)}, f32[128,2048]{1,0:T(8,128)}, f32[256,768]{1,0:T(8,128)}, f32[64,1024]{1,0:T(8,128)}, f32[512,256]{1,0:T(8,1...) custom-call(bf16[512,2048]{1,0:T(8,128)(2,1)} %get-tuple-element.61., ...), custom_call_target="tpu_custom_call" | custom-call | tf_op jit(solution)/shard_map/weight_pass/pallas_call | solution.py:2806
  545.2 1.3 slice.34
  546.5 1.5 fusion
  548.0 1.0 slice.32
  549.0 1.2 slice.31
  550.2 1.0 copy.40
  552.0 1.2 pad_maximum_fusion.2
  553.2 1.1 copy.38
  554.4 3.0 convert_bitcast_fusion
  558.2 1.0 copy.52
  561.6 0.9 copy.56
  563.3 2.9 copy.58
  566.4 1.2 slice-done.1
  567.6 2.9 copy.59
  570.5 1.4 slice-done.5
  572.0 2.5 copy.60
  (48 shorter events, 6.8 us)
Async XLA Ops:
  0.6 3.9 copy-start.8
  3.6 3.2 copy-start
  549.0 5.4 copy-start.1
  554.4 3.0 copy-start.7
  554.4 3.8 copy-start.2
  554.4 4.8 copy-start.9
  554.4 8.9 %slice-start.2 = ((s8[5767168]{0:T(1024)(128)(4,1)}), s8[4194304]{0:T(1024)(128)(4,1)S(1)}, s32[]{:S(2)}) async-start(s8[5767168]{0:T(1024)(128)(4,1)} %bitcast.65), calls=%async_computation.2 | async-start | bytes 8388608
  557.4 2.5 copy-start.6
  557.4 3.3 copy-start.5
  557.4 4.2 copy-start.4
  557.4 5.9 %slice-start.3 = ((s8[5767168]{0:T(1024)(128)(4,1)}), s8[1572864]{0:T(1024)(128)(4,1)S(1)}, s32[]{:S(2)}) async-start(s8[5767168]{0:T(1024)(128)(4,1)} %bitcast.65), calls=%async_computation.3 | async-start | bytes 3145728
  558.2 4.2 copy-start.3
  562.4 4.0 slice-start
  563.3 4.3 slice-start.1
  563.3 7.2 %slice-start.4 = ((s8[5767168]{0:T(1024)(128)(4,1)}), s8[1572864]{0:T(1024)(128)(4,1)S(1)}, s32[]{:S(2)}) async-start(s8[5767168]{0:T(1024)(128)(4,1)} %bitcast.68), calls=%async_computation.4 | async-start | bytes 3145728
  567.6 4.4 slice-start.5
where the time goes:
time: 585 us; the launch traced here: 575 us
  Pallas kernels  537 us (92%)
  local copies, waits for them, and re-layouts  29.3 us (5%)
  other arithmetic  7.78 us (1%)
    pallas_call x1, Pallas kernels, moe_pass(): pl.pallas_call(functools.partial(moe_kernel, expert_width=expert_width, r...  167 us
    pallas_call x1, Pallas kernels, front_pass(): pl.pallas_call(front_kernel, out_shape=(array(group_rows, width), array(g...  137 us
    pallas_call x1, Pallas kernels, back_pass(): pl.pallas_call(back_kernel, out_shape=(array(ranks, rows, width), array(r...  127 us
    pallas_call x1, Pallas kernels, weight_pass(): pl.pallas_call(weight_kernel, out_shape=(jax.ShapeDtypeStruct((rows, widt...  106 us
    unnamed x44, local copies, waits for them, and re-layouts  19.4 us

commit v1 on v0

--- a/solution.py
+++ b/solution.py
@@ -1148,7 +1148,7 @@
     expert_down,
     routes,
     route_gates,
-    latent_rows,
+    latent_columns,
     attn_gain,
     latent_gain,
     mlp_gain,
@@ -1177,6 +1177,7 @@
     expand_all,
     output_all,
     down_rows,
+    latent_rows,
     normed,
     latent_low,
     q_cat,
@@ -1386,6 +1387,14 @@
         ),
         pltpu.make_async_copy(cotangent, cotan_all.at[0, 0], local_sem.at[5]),
         pltpu.make_async_copy(expert_down, down_rows.at[pl.ds(0, routed_width)], local_sem.at[6]),
+        pltpu.make_async_copy(
+            latent_columns, latent_rows.at[pl.ds(0, LATENT + ROPE)], local_sem.at[18]
+        ),
+        pltpu.make_async_copy(
+            latent_columns.at[pl.ds(LATENT, ROPE)],
+            latent_rows.at[pl.ds(LATENT + ROPE, ROPE)],
+            local_sem.at[19],
+        ),
     ]
     for copy in local:
         copy.start()
@@ -1513,6 +1522,8 @@
     weight_last(1)
     local[1].wait()
     local[2].wait()
+    local[7].wait()
+    local[8].wait()
     project_piece(0)
     project_piece(1)
     weight_far(2)
@@ -1637,7 +1648,7 @@
     expert_down,
     routes,
     route_gates,
-    latent_rows,
+    latent_columns,
     attn_gain,
     latent_gain,
     mlp_gain,
@@ -1692,7 +1703,8 @@
             array(*by_slot, width),
             array(*by_slot, hidden_width),
         ),
-        in_specs=[pl.BlockSpec(memory_space=pltpu.SMEM)] + [anywhere] * 7 + [in_vmem] * 7,
+        in_specs=[pl.BlockSpec(memory_space=pltpu.SMEM)] + [anywhere] * 7
+        + [in_vmem] * 2 + [anywhere] + [in_vmem] * 4,
         out_specs=(anywhere, anywhere, in_vmem)
         + (anywhere,) * 8
         + (in_vmem,) * 4
@@ -1703,6 +1715,7 @@
             pltpu.VMEM(full_expand(), low),
             pltpu.VMEM(full_output(), low),
             pltpu.VMEM((hidden_width, width), low),
+            pltpu.VMEM((LATENT + 2 * ROPE, width), low),
             pltpu.VMEM((group_rows, width), low),
             pltpu.VMEM((group_rows, LATENT), low),
             pltpu.VMEM((heads, group_rows, NOPE + lanes), low),
@@ -1718,7 +1731,7 @@
             pltpu.VMEM((2, 2, rows, hidden_width), low),
             pltpu.VMEM((ranks - 1, rows, width), low),
             pltpu.VMEM((ranks - 1, rows, width), low),
-            dma((18,)),
+            dma((20,)),
             dma((2,)),
             dma((2,)),
             dma((2,)),
@@ -1752,7 +1765,7 @@
         expert_down,
         routes,
         route_gates,
-        latent_rows,
+        latent_columns,
         attn_gain,
         latent_gain,
         mlp_gain,
@@ -2047,7 +2060,7 @@
     outputs(1)
     sums_next(0)
     sums_first(1)
-    products(0, 0, 3)
+    products(0, 0, 4)
     resid_step(1).wait_recv()
     resid_step(2).start()
     attended_piece(2)
@@ -2055,7 +2068,7 @@
     outputs(2)
     sums_next(1)
     sums_first(2)
-    products(0, 3, 5)
+    products(0, 4, 6)
     resid_step(2).wait_recv()
     save = pltpu.make_async_copy(resid_buf, resid_all, local_sem.at[3])
     save.start()
@@ -2084,16 +2097,17 @@
         outputs(3)
         sums_next(2)
         sums_first(3)
-        products(0, 5, 8)
+        products(0, 6, 12)
 
     def between_1():
         sums_last(2)
         sums_next(3)
-        products(0, 8, 16)
+        products(0, 12, 16)
+        products(1, 0, 6)
 
     def between_2():
         sums_last(3)
-        products(1, 0, 8)
+        products(1, 6, 16)
 
     for step, between in enumerate((between_0, between_1, between_2)):
         values = partial(step + 1)
@@ -2114,7 +2128,6 @@
     latent_back[:, LATENT:] = parts[2] + ring_buf[ranks - 2, :, width + LATENT :].astype(
         jnp.float32
     )
-    products(1, 8, 16)
     save.wait()
     for step in range(ranks - 1):
         resid_step(step).wait_send()
@@ -2712,14 +2725,14 @@
     sums_first(2)
     sums_first(1)
     latent_sum()
-    products(0, 3)
+    products(0, 6)
     moe_next(1)
     latent_cube()
     sums_next(0)
     sums_next(2)
     sums_next(1)
     gains_first()
-    products(3, 5)
+    products(6, 12)
     latent_forward()
     moe_next(2)
     latent_far()
@@ -2727,11 +2740,10 @@
     shared_low[0:2] = bfloat(shared_full[...])
     for copy in shared_copies(pair, 0) + [own_shared(pair, 0)]:
         copy.start()
-    products(5, 8)
+    products(12, 16)
     for i in (0, 2, 1):
         sums_last(i)
     gains_last()
-    products(8, 16)
     for copy in shared_copies(single, 1) + [own_shared(single, 1)]:
         copy.start()
     moe_last()
@@ -3006,7 +3018,7 @@
         expert_down.reshape(-1, width),
         routes.T,
         route_gates.T,
-        jnp.concatenate([latent_columns, latent_columns[LATENT:]], axis=0),
+        latent_columns,
         attn_gain[None],
         latent_gain[None],
         mlp_gain[None],

time: 585 us -> 558 us (0.954)
  Pallas kernels: 537 us -> 513 us
    pallas_call x1, Pallas kernels: 106 us -> 88.4 us  [weight_pass(): pl.pallas_call(weight_kernel, out_shape=(jax.ShapeDtypeStruct((rows, widt...]
    unnamed x44 -> x46, local copies, waits for them, and re-layouts: 19.4 us -> 19.4 us
where the time goes in v1:
time: 558 us; the launch traced here: 548 us
  Pallas kernels  513 us (92%)
  local copies, waits for them, and re-layouts  27.2 us (5%)
  other arithmetic  6.11 us (1%)
    pallas_call x1, Pallas kernels, moe_pass(): pl.pallas_call(functools.partial(moe_kernel, expert_width=expert_width, r...  167 us
    pallas_call x1, Pallas kernels, front_pass(): pl.pallas_call(front_kernel, out_shape=(array(group_rows, width), array(g...  136 us
    pallas_call x1, Pallas kernels, back_pass(): pl.pallas_call(back_kernel, out_shape=(array(ranks, rows, width), array(r...  122 us
    pallas_call x1, Pallas kernels, weight_pass(): pl.pallas_call(weight_kernel, out_shape=(jax.ShapeDtypeStruct((rows, widt...  88.4 us
    unnamed x46, local copies, waits for them, and re-layouts  19.4 us

profile of v1, /device:TPU:9, one launch (start us, length us, event | category | flops | bytes accessed | tf_op | source)
XLA Modules:
  0.0 548.0 jit_solution(2286905187470004658)
XLA Ops:
  1.3 1.2 copy.33
  3.7 1.1 pad_maximum_fusion.shared
  4.8 136.4 %front_pass.1 = (bf16[512,2048]{1,0:T(8,128)(2,1)}, bf16[512,512]{1,0:T(8,128)(2,1)}, f32[128,512]{1,0:T(8,128)}, bf16[2048,768]{1,0:T(8,128)(2,1)}, bf16[512,10...) custom-call(s32[1,3]{1,0:T(1,128)} %lengths.1, ...), custom_call_target="tpu_custom_call" | custom-call | tf_op jit(solution)/shard_map/front_pass/pallas_call | solution.py:1683
  141.2 166.9 %moe_pass.1 = (bf16[8,4,128,2048]{3,2,1,0:T(8,128)(2,1)}, bf16[8,4,128,896]{3,2,1,0:T(8,128)(2,1)}, bf16[8,4,128,896]{3,2,1,0:T(8,128)(2,1)}, bf16[8,4,128,896]{...) custom-call(bf16[128,2048]{1,0:T(8,128)(2,1)} %get-tuple-element.64.rows, ...), custom_call_target="tpu_custom_call" | custom-call | tf_op jit(solution)/shard_map/moe_pass/pallas_call | solution.py:1050
  308.1 121.7 %back_pass.1 = (bf16[4,128,2048]{2,1,0:T(8,128)(2,1)}, bf16[4,128,2048]{2,1,0:T(8,128)(2,1)}, f32[704,2048]{1,0:T(8,128)}, f32[704,2048]{1,0:T(8,128)}, f32[2,96...) custom-call(bf16[128,2048]{1,0:T(8,128)(2,1)} %get-tuple-element.69., ...), custom_call_target="tpu_custom_call" | custom-call | tf_op jit(solution)/shard_map/back_pass/pallas_call | solution.py:2169
  429.8 88.4 %weight_pass.1 = (bf16[128,2048]{1,0:T(8,128)(2,1)}, f32[128,2048]{1,0:T(8,128)}, f32[256,768]{1,0:T(8,128)}, f32[64,1024]{1,0:T(8,128)}, f32[512,256]{1,0:T(8,1...) custom-call(bf16[512,2048]{1,0:T(8,128)(2,1)} %get-tuple-element.61., ...), custom_call_target="tpu_custom_call" | custom-call | tf_op jit(solution)/shard_map/weight_pass/pallas_call | solution.py:2818
  518.2 1.3 slice.30
  519.5 1.5 fusion
  521.1 1.0 slice.28
  522.0 1.2 slice.27
  523.3 1.0 copy.40
  524.3 0.8 copy.36
  525.1 1.2 pad_maximum_fusion.1
  526.3 1.1 copy.38
  527.4 3.0 convert_bitcast_fusion
  531.3 1.0 copy.52
  533.8 0.9 copy.55
  534.6 0.9 copy.56
  535.5 0.9 copy.57
  536.4 2.9 copy.58
  539.5 1.2 slice-done.1
  540.7 2.9 copy.59
  543.6 1.4 slice-done.5
  545.0 2.5 copy.60
  (48 shorter events, 4.3 us)
Async XLA Ops:
  0.6 2.9 copy-start.8
  0.7 2.9 copy-start.9
  0.7 2.9 copy-start.7
  522.0 5.4 copy-start
  527.4 3.0 copy-start.6
  527.4 3.8 copy-start.1
  527.4 4.8 copy-start.10
  527.4 8.9 %slice-start.2 = ((s8[5767168]{0:T(1024)(128)(4,1)}), s8[4194304]{0:T(1024)(128)(4,1)S(1)}, s32[]{:S(2)}) async-start(s8[5767168]{0:T(1024)(128)(4,1)} %bitcast.64), calls=%async_computation.2 | async-start | bytes 8388608
  530.5 2.5 copy-start.5
  530.5 3.3 copy-start.4
  530.5 4.2 copy-start.3
  530.5 5.9 %slice-start.3 = ((s8[5767168]{0:T(1024)(128)(4,1)}), s8[1572864]{0:T(1024)(128)(4,1)S(1)}, s32[]{:S(2)}) async-start(s8[5767168]{0:T(1024)(128)(4,1)} %bitcast.64), calls=%async_computation.3 | async-start | bytes 3145728
  531.3 4.2 copy-start.2
  535.5 4.0 slice-start
  536.3 4.3 slice-start.1
  536.4 7.2 %slice-start.4 = ((s8[5767168]{0:T(1024)(128)(4,1)}), s8[1572864]{0:T(1024)(128)(4,1)S(1)}, s32[]{:S(2)}) async-start(s8[5767168]{0:T(1024)(128)(4,1)} %bitcast.67), calls=%async_computation.4 | async-start | bytes 3145728
  540.6 4.4 slice-start.5
